TPU v7x, 32 devices: a whole 2x2x4 slice. The times are simulated.
32 devices in a mesh: groups: 2 (over y), seq: 8 (over z, x), head: 2 (over core).
Axes of the slice: x: 2, y: 2, z: 4, core: 2. Of those that a mesh axis runs over, the one named last changes fastest.
Arguments:
- query_states: bfloat16 [2048, 1536], P(('groups', 'seq'), 'head'), parts along dimension 0, may hold values from -8 to 8
- key_states: bfloat16 [2048, 1536], P(('groups', 'seq'), 'head'), parts along dimension 0, may hold values from -8 to 8
- value_states: bfloat16 [2048, 1536], P(('groups', 'seq'), 'head'), parts along dimension 0, may hold values from -6 to 6
- d_attended: bfloat16 [2048, 1536], P(('groups', 'seq'), 'head'), parts along dimension 0, may hold values from -6 to 6
- ctrl_key: bfloat16 [512, 1536], P(('groups', 'seq'), 'head'), parts along dimension 0, may hold values from -6 to 6
- ctrl_value: bfloat16 [512, 1536], P(('groups', 'seq'), 'head'), parts along dimension 0, may hold values from -6 to 6
- ctrl_bias: float32 [24], P('head'), may hold values from 0.5 to 3
- tube_lengths: int32 [8], P('groups'), parts along dimension 0, may hold values from 1 to 3, as said below
- tube_owner: int32 [8], P('groups'), parts along dimension 0, may hold values from 0 to 7
- ctrl_owner: int32 [512], P('groups'), parts along dimension 0, may hold values from 0 to 7
Outputs:
- attended: bfloat16 [2048, 1536], P(('groups', 'seq'), 'head'), parts along dimension 0
- d_query: bfloat16 [2048, 1536], P(('groups', 'seq'), 'head'), parts along dimension 0
- d_key: bfloat16 [2048, 1536], P(('groups', 'seq'), 'head'), parts along dimension 0
- d_value: bfloat16 [2048, 1536], P(('groups', 'seq'), 'head'), parts along dimension 0
- d_ctrl_key: bfloat16 [512, 1536], P(('groups', 'seq'), 'head'), parts along dimension 0
- d_ctrl_value: bfloat16 [512, 1536], P(('groups', 'seq'), 'head'), parts along dimension 0
There are 2 independent parts, one for each index of `groups`. A program takes and returns all parts, laid end to end along the dimension named above; an argument that names none is the same for every part. Nothing has to cross between parts.
Inputs may be any that keep to these rules, and one draw needn't show every extreme that they name: Tube t is the run of tube_lengths[t] consecutive blocks of 128 tokens after the blocks of the tubes before it; the lengths sum to 8 and the longest has exactly 3 blocks.
All inputs are finite; a program needn't handle non-finite values.
Results may differ from a plain program's by a relative error of at most 0.015.
Values may be sent and summed in bfloat16 or wider, within the bound.
A program may use at most 64 MiB of HBM per device.

v0:
```python
from functools import partial

import jax
import jax.numpy as jnp
from jax import lax
from jax.sharding import PartitionSpec as P

BLK = 128
REACH = 2


MASKED = -1e30


def passed_along(block, axis, distance):
    devices = range(lax.axis_size(axis))
    route = [(i - distance, i) for i in devices if i - distance in devices]
    return lax.ppermute(block, axis, route)


def tube_tables(tube_lengths, tube_owner, blocks_all):
    tube_ends = jnp.cumsum(tube_lengths, dtype=jnp.int32)
    blocks = jnp.arange(blocks_all, dtype=jnp.int32)
    tube_index = jnp.sum(
        (tube_ends[None, :] <= blocks[:, None]).astype(jnp.int32), axis=1, dtype=jnp.int32
    )
    tube_ids = jnp.arange(tube_lengths.shape[0], dtype=jnp.int32)
    matches = tube_ids[None, :] == tube_index[:, None]
    owner_index = jnp.sum(jnp.where(matches, tube_owner[None, :], 0), axis=1, dtype=jnp.int32)
    return (tube_index, owner_index)


def split_heads(rows_in, head_width):
    return rows_in.reshape(rows_in.shape[0], rows_in.shape[1] // head_width, head_width)


def scores_of(q_blk, k_blk):
    return jnp.einsum(
        "qhd,khd->hqk", q_blk, k_blk, preferred_element_type=jnp.float32
    ) * q_blk.shape[-1] ** (-0.5)


def weights_of(scores, row_high, row_total):
    return jnp.exp(scores - row_high[..., None]) / row_total[..., None]


def raise_stats(statistics, scores):
    row_high, row_total = statistics
    new_high = jnp.maximum(row_high, jnp.max(scores, axis=-1))
    row_total = row_total * jnp.exp(row_high - new_high) + jnp.sum(
        jnp.exp(scores - new_high[..., None]), axis=-1
    )
    return (new_high, row_total)


def unchanged(carried):
    return carried


def round_trip(values):
    return lax.optimization_barrier(values.astype(jnp.bfloat16)).astype(jnp.float32)


def shards(
    query_states,
    key_states,
    value_states,
    d_attended,
    ctrl_key,
    ctrl_value,
    ctrl_bias,
    tube_lengths,
    tube_owner,
    ctrl_owner,
):
    row_count, width_all = query_states.shape
    head_width = width_all // ctrl_bias.shape[0]
    head_scale = head_width ** (-0.5)
    per_device = row_count // BLK
    blocks_all = lax.axis_size("seq") * per_device
    position = lax.axis_index("seq")
    slot_count = 2 * REACH + 1
    tube_index, owner_index = tube_tables(tube_lengths, tube_owner, blocks_all)
    ctrl_pair = lax.all_gather(jnp.stack([ctrl_key, ctrl_value]), "seq", axis=1, tiled=True)
    ctrl_keys = split_heads(ctrl_pair[0], head_width)
    ctrl_values = split_heads(ctrl_pair[1], head_width)
    ctrl_shift = ctrl_bias[:, None, None]
    key_value = jnp.stack([key_states, value_states])
    lower_side = [passed_along(key_value, "seq", distance) for distance in range(REACH, 0, -1)]
    upper_side = [passed_along(key_value, "seq", -distance) for distance in range(1, REACH + 1)]
    kv_window = lower_side + [key_value] + upper_side

    def member(slot_index, block_local, tube_id):
        block_id = (position - REACH + slot_index) * per_device + block_local
        clipped = jnp.clip(block_id, 0, blocks_all - 1)
        return (block_id >= 0) & (block_id < blocks_all) & (tube_index[clipped] == tube_id)

    def window_block(window, slot_index, block_local, member_index):
        return split_heads(
            window[slot_index][member_index, block_local * BLK : (block_local + 1) * BLK],
            head_width,
        )

    def visit_keys(update, carried, tube_id, skipped):
        for slot_index in range(slot_count):
            for key_local in range(per_device):
                if slot_index == REACH and key_local == skipped:
                    continue
                carried = lax.cond(
                    member(slot_index, key_local, tube_id),
                    partial(update, slot_index=slot_index, key_local=key_local),
                    unchanged,
                    carried,
                )
        return carried

    q_blocks, g_blocks, query_tubes, ctrl_masks = ([], [], [], [])
    query_local = 0
    q_blocks.append(split_heads(query_states, head_width))
    g_blocks.append(split_heads(d_attended, head_width))
    block_id = position * per_device + query_local
    query_tubes.append(tube_index[block_id])
    ctrl_masks.append((ctrl_owner == owner_index[block_id])[None, None, :])

    def ctrl_scores(query_local):
        return jnp.where(
            ctrl_masks[query_local],
            scores_of(q_blocks[query_local], ctrl_keys) + ctrl_shift,
            MASKED,
        )

    highs, totals, deltas, attended_blocks = ([], [], [], [])
    query_local = 0
    q_blk = q_blocks[query_local]
    own_scores = scores_of(q_blk, window_block(kv_window, REACH, query_local, 0))
    row_high = jnp.max(own_scores, axis=-1)
    statistics = (row_high, jnp.sum(jnp.exp(own_scores - row_high[..., None]), axis=-1))
    statistics = raise_stats(statistics, ctrl_scores(query_local))

    def add_stats(carried, slot_index, key_local, q_blk=q_blk):
        return raise_stats(
            carried, scores_of(q_blk, window_block(kv_window, slot_index, key_local, 0))
        )

    row_high, row_total = visit_keys(add_stats, statistics, query_tubes[query_local], query_local)
    ctrl_weights = weights_of(ctrl_scores(query_local), row_high, row_total).astype(jnp.bfloat16)
    summed = jnp.einsum(
        "hqk,khd->qhd", ctrl_weights, ctrl_values, preferred_element_type=jnp.float32
    )

    def add_values(
        carried, slot_index, key_local, q_blk=q_blk, row_high=row_high, row_total=row_total
    ):
        k_blk = window_block(kv_window, slot_index, key_local, 0)
        v_blk = window_block(kv_window, slot_index, key_local, 1)
        weights = weights_of(scores_of(q_blk, k_blk), row_high, row_total).astype(jnp.bfloat16)
        return carried + jnp.einsum(
            "hqk,khd->qhd", weights, v_blk, preferred_element_type=jnp.float32
        )

    summed = visit_keys(add_values, summed, query_tubes[query_local], -1)
    attended_blk = summed.astype(jnp.bfloat16)
    row_delta = jnp.sum(
        g_blocks[query_local].astype(jnp.float32) * attended_blk.astype(jnp.float32), axis=-1
    ).T
    highs.append(row_high)
    totals.append(row_total)
    deltas.append(row_delta)
    attended_blocks.append(attended_blk)

    def grad_terms(query_local, v_blk, scores):
        weights = weights_of(scores, highs[query_local], totals[query_local])
        d_prob = jnp.einsum(
            "qhd,khd->hqk", g_blocks[query_local], v_blk, preferred_element_type=jnp.float32
        )
        d_scores = (weights * (d_prob - deltas[query_local][..., None])).astype(jnp.bfloat16)
        return (weights.astype(jnp.bfloat16), d_scores)

    query_local = 0
    rounded, d_scores = grad_terms(query_local, ctrl_values, ctrl_scores(query_local))
    d_queries = [
        jnp.einsum("hqk,khd->qhd", d_scores, ctrl_keys, preferred_element_type=jnp.float32)
        * head_scale
    ]
    ctrl_key_grad = (
        jnp.einsum(
            "hqk,qhd->khd", d_scores, q_blocks[query_local], preferred_element_type=jnp.float32
        )
        * head_scale
    )
    ctrl_value_grad = jnp.einsum(
        "hqk,qhd->khd", rounded, g_blocks[query_local], preferred_element_type=jnp.float32
    )
    block_zeros = jnp.zeros((BLK, width_all // head_width, head_width), jnp.float32)
    key_parts = jnp.zeros((2, row_count, width_all), jnp.float32)
    for slot_index in range(slot_count):
        key_local = 0
        k_blk = window_block(kv_window, slot_index, key_local, 0)
        v_blk = window_block(kv_window, slot_index, key_local, 1)
        key_grad = block_zeros
        value_grad = block_zeros
        query_local = 0

        def add_grads(carried, query_local=query_local, k_blk=k_blk, v_blk=v_blk):
            rounded, d_scores = grad_terms(
                query_local, v_blk, scores_of(q_blocks[query_local], k_blk)
            )
            d_query_blk = (
                carried[0]
                + jnp.einsum("hqk,khd->qhd", d_scores, k_blk, preferred_element_type=jnp.float32)
                * head_scale
            )
            key_term = (
                jnp.einsum(
                    "hqk,qhd->khd",
                    d_scores,
                    q_blocks[query_local],
                    preferred_element_type=jnp.float32,
                )
                * head_scale
            )
            value_term = jnp.einsum(
                "hqk,qhd->khd", rounded, g_blocks[query_local], preferred_element_type=jnp.float32
            )
            return (d_query_blk, key_term, value_term)

        carried = lax.cond(
            member(slot_index, key_local, query_tubes[query_local]),
            add_grads,
            unchanged,
            (d_queries[query_local], key_grad, value_grad),
        )
        d_queries[query_local], key_grad, value_grad = carried
        slot_pieces = jnp.stack([key_grad, value_grad]).reshape(2, BLK, width_all)
        if slot_index == REACH:
            key_parts = key_parts + round_trip(slot_pieces)
        else:
            received = passed_along(slot_pieces.astype(jnp.bfloat16), "seq", slot_index - REACH)
            key_parts = key_parts + received.astype(jnp.float32)
    key_results = key_parts.astype(jnp.bfloat16)
    ctrl_terms = jnp.stack(
        [ctrl_key_grad.reshape(-1, width_all), ctrl_value_grad.reshape(-1, width_all)]
    )
    ctrl_results = lax.psum_scatter(ctrl_terms, "seq", scatter_dimension=1, tiled=True).astype(
        jnp.bfloat16
    )
    attended = attended_blocks[0].reshape(row_count, width_all)
    d_query = d_queries[0].reshape(row_count, width_all).astype(jnp.bfloat16)
    return (attended, d_query, key_results[0], key_results[1], ctrl_results[0], ctrl_results[1])


def solution(mesh):
    return jax.shard_map(
        shards,
        mesh=mesh,
        in_specs=(
            P(("groups", "seq"), "head"),
            P(("groups", "seq"), "head"),
            P(("groups", "seq"), "head"),
            P(("groups", "seq"), "head"),
            P(("groups", "seq"), "head"),
            P(("groups", "seq"), "head"),
            P("head"),
            P("groups"),
            P("groups"),
            P("groups"),
        ),
        out_specs=(
            P(("groups", "seq"), "head"),
            P(("groups", "seq"), "head"),
            P(("groups", "seq"), "head"),
            P(("groups", "seq"), "head"),
            P(("groups", "seq"), "head"),
            P(("groups", "seq"), "head"),
        ),
        check_vma=False,
    )
```

profile of v0, /device:TPU:0, one launch (start us, length us, event | category | flops | bytes accessed | tf_op | source)
XLA Modules:
  0.0 172.5 jit_solution(9648057972593388765)
XLA Ops:
  7.2 1.1 copy.84
  8.3 1.2 copy.86
  9.5 0.8 pad_maximum_fusion.1
  10.3 5.7 %collective-permute-start = (bf16[2,128,768]{1,2,0:T(8,128)(2,1)}, bf16[2,128,768]{1,2,0:T(8,128)(2,1)}, u32[]{:S(2)}, u32[]{:S(2)}) collective-permute-start(bf16[2,128,768]{1,2,0:T(8,128)(2,1)} %pad_maximum_fusion.1), channel_id=1, source_target_pairs={{0,4},{2,6},{4,8},{6,10},{8,12},{10,14},{1,5},{3,7},{5,9},{7,11},{... | collective-permute-start | bytes 1179656 | tf_op jit(solution)/shard_map/ppermute | solution.py:18
  16.0 4.1 %collective-permute-start.1 = (bf16[2,128,768]{1,2,0:T(8,128)(2,1)}, bf16[2,128,768]{1,2,0:T(8,128)(2,1)}, u32[]{:S(2)}, u32[]{:S(2)}) collective-permute-start(bf16[2,128,768]{1,2,0:T(8,128)(2,1)} %pad_maximum_fusion.1), channel_id=1, source_target_pairs={{0,2},{2,4},{4,6},{6,8},{8,10},{10,12},{12,14},{1,3},{3,5},{5,7},{... | collective-permute-start | bytes 1179656 | tf_op jit(solution)/shard_map/ppermute | solution.py:18
  20.1 1.3 collective-permute-start.2
  21.4 1.3 collective-permute-start.3
  23.0 0.6 fusion.111
  30.2 35.6 %all_gather.3 = bf16[2,256,768]{2,1,0:T(8,128)(2,1)S(1)} all-gather(bf16[2,32,768]{2,1,0:T(8,128)(2,1)S(1)} %pad_maximum_fusion.7), channel_id=1, replica_groups=mesh['groups'=2,'seq'=8,'head'=2] {'seq'}, dimensions={1}, use_global_device_ids=true | all-gather | bytes 884736 | tf_op jit(solution)/shard_map/all_gather | solution.py:84
  65.8 0.9 copy.81
  67.2 0.6 dynamic_slice.36
  68.2 0.7 broadcast_compare_fusion
  68.8 0.6 bitcast_reduce_fusion
  69.8 0.6 multiply_add_fusion.4
  70.7 2.8 %conditional.21 = ((f32[12,128]{1,0:T(8,128)S(1)}, f32[12,128]{1,0:T(8,128)})) conditional(s32[]{:T(128)} %convert_element_type.133, (f32[12,128]{1,0:T(8,128)S(1)}, f32[12,128]{1,0:T(8,128)}) %get-tuple-element.580, (bf16[2,128,768]{1,2,0:T(8,128)(2,1)}, bf16[128,12,64]{0,2,1:T(8,128)(2,1)S(1)}, f32[12,128]{1,0:T(8,128)S(1)}, ...), branch_computations={%region_15.16_spmd, %region_16.19_spmd} | conditional | flops 25955328 | bytes 2439192 | solution.py:109
  70.7 0.9 slice.62
  72.1 1.3 multiply_add_fusion.2
  73.4 1.8 %conditional.22 = ((f32[12,128]{1,0:T(8,128)S(1)}, f32[12,128]{1,0:T(8,128)})) conditional(s32[]{:T(128)} %convert_element_type.132, (f32[12,128]{1,0:T(8,128)S(1)}, f32[12,128]{1,0:T(8,128)}) %get-tuple-element.581, (bf16[2,128,768]{1,2,0:T(8,128)(2,1)S(1)}, bf16[128,12,64]{0,2,1:T(8,128)(2,1)S(1)}, f32[12,128]{1,0:T(8,128)S(1)}, ...), branch_computations={%region_19.20_spmd, %region_20.23_spmd} | conditional | flops 25955328 | bytes 2439192 | solution.py:109
  73.9 1.3 multiply_add_fusion.3
  75.3 1.0 fusion.96
  76.6 5.3 %conditional.25 = (f32[128,12,64]{0,2,1:T(8,128)S(1)}) conditional(s32[]{:T(128)} %convert_element_type.134, f32[128,12,64]{0,2,1:T(8,128)S(1)} %get-tuple-element.584, (bf16[128,768]{1,0:T(8,128)(2,1)}, bf16[128,12,64]{0,2,1:T(8,128)(2,1)S(1)}, f32[12,128]{1,0:T(8,128)S(1)}, f32[12,128]{1,0:T(8,128)}, bf16[128,768]{1,0:T(8,128)(2,1)}, ...), branch_computations={%region_27.28_spmd, %region_28.29_spmd} | conditional | flops 51216384 | bytes 2174984 | solution.py:109
  76.6 1.7 %copy.89 = bf16[128,768]{0,1:T(8,128)(2,1)} copy(bf16[128,768]{1,0:T(8,128)(2,1)} %get-tuple-element.460) | data formatting | bytes 393216 | tf_op jit(solution)/shard_map
  78.4 1.7 %copy.88 = bf16[128,768]{0,1:T(8,128)(2,1)} copy(bf16[128,768]{1,0:T(8,128)(2,1)} %get-tuple-element.456) | data formatting | bytes 393216 | tf_op jit(solution)/shard_map
  80.1 1.8 %fusion.22 = f32[128,12,64]{0,2,1:T(8,128)S(1)} fusion(f32[128,12,64]{0,2,1:T(8,128)S(1)} %get-tuple-element.258, bf16[128,12,64]{0,2,1:T(8,128)(2,1)} %bitcast.305, bf16[128,12,64]{0,2,1:T(8,128)(2,1)S(1)} %get-tuple-element.259, bf16[128,12,64]{0,2,1:T(8,128)(2,1)} %bitcast.306, f32[12,128]{1,0:T(8,128)} %get-tuple-element.262, ...), kind=kOutput, calls=%fused_computation.40 | convolution fusion | flops 51216384 | bytes 1388544 | tf_op jit(solution)/shard_map/cond/branch_1_fun/hqk,khd->qhd/dot_general | solution.py:157
  81.9 3.6 %conditional.26 = (f32[128,12,64]{0,2,1:T(8,128)S(1)}) conditional(s32[]{:T(128)} %convert_element_type.133, f32[128,12,64]{0,2,1:T(8,128)S(1)} %get-tuple-element.585, (bf16[2,128,768]{1,2,0:T(8,128)(2,1)}, bf16[128,12,64]{0,2,1:T(8,128)(2,1)S(1)}, f32[12,128]{1,0:T(8,128)S(1)}, f32[12,128]{1,0:T(8,128)}, f32[128,12,64]{0,2,1:T(8,128)S(1)}) %tuple.278), branch_computations={%region_29.30_spmd, %region_30.31_spmd} | conditional | flops 51216384 | bytes 2174984 | solution.py:109
  82.0 1.8 %fusion.103 = (bf16[1,128,768]{1,2,0:T(8,128)(2,1)}, bf16[1,128,768]{1,2,0:T(8,128)(2,1)}) fusion(bf16[2,128,768]{1,2,0:T(8,128)(2,1)} %get-tuple-element.266), kind=kLoop, calls=%fused_computation.180 | loop fusion | bytes 786432 | tf_op jit(solution)/shard_map/cond/branch_1_fun/slice | solution.py:100
  83.7 1.8 %fusion.31 = f32[128,12,64]{0,2,1:T(8,128)S(1)} fusion(f32[128,12,64]{0,2,1:T(8,128)S(1)} %get-tuple-element.264, bf16[128,12,64]{0,2,1:T(8,128)(2,1)} %bitcast.314, bf16[128,12,64]{0,2,1:T(8,128)(2,1)S(1)} %get-tuple-element.265, bf16[128,12,64]{0,2,1:T(8,128)(2,1)} %bitcast.313, f32[12,128]{1,0:T(8,128)} %get-tuple-element.268, ...), kind=kOutput, calls=%fused_computation.51 | convolution fusion | flops 51216384 | bytes 1388544 | tf_op jit(solution)/shard_map/cond/branch_1_fun/hqk,khd->qhd/dot_general | solution.py:157
  85.6 2.8 %conditional.27 = (f32[128,12,64]{0,2,1:T(8,128)S(1)}, bf16[128,768]{1,0:T(8,128)(2,1)S(1)}) conditional(s32[]{:T(128)} %convert_element_type.132, f32[128,12,64]{0,2,1:T(8,128)S(1)} %get-tuple-element.586, (bf16[2,128,768]{1,2,0:T(8,128)(2,1)S(1)}, bf16[128,12,64]{0,2,1:T(8,128)(2,1)S(1)}, f32[12,128]{1,0:T(8,128)S(1)}, f32[12,128]{1,0:T(8,128)}, ...), branch_computations={%region_31.32_spmd, %region_32.33_spmd} | conditional | flops 51314688 | bytes 2764816
  85.6 0.8 fusion.104
  86.4 1.8 %fusion.105 = (bf16[128,12,64]{0,2,1:T(8,128)(2,1)S(1)}, f32[128,12,64]{0,2,1:T(8,128)S(1)}) fusion(f32[128,12,64]{0,2,1:T(8,128)S(1)} %get-tuple-element.269, bf16[128,12,64]{0,2,1:T(8,128)(2,1)} %bitcast.308, bf16[128,12,64]{0,2,1:T(8,128)(2,1)S(1)} %get-tuple-element.270, bf16[128,12,64]{0,2,1:T(8,128)(2,1)} %bitcast.307, ...), kind=kOutput, calls=%fused_computation.182 | convolution fusion | flops 51314688 | bytes 1585152 | tf_op jit(solution)/shard_map/cond/branch_1_fun/hqk,khd->qhd/dot_general | solution.py:157
  88.4 1.3 fusion.113
  89.8 1.4 fusion.90
  91.4 0.4 convolution_multiply_fusion.24
  92.1 1.3 pad_maximum_fusion
  93.4 1.0 copy-done.7
  94.9 0.8 copy-done.2
  95.9 3.7 %conditional.30 = (f32[128,12,64]{0,2,1:T(8,128)S(1)}, bf16[1,128,768]{2,1,0:T(8,128)(2,1)S(1)}, bf16[1,128,768]{2,1,0:T(8,128)(2,1)S(1)}) conditional(s32[]{:T(128)} %convert_element_type.134, f32[128,12,64]{0,2,1:T(8,128)S(1)} %get-tuple-element.352, (bf16[128,12,64]{0,2,1:T(8,128)(2,1)S(1)}, bf16[128,12,64]{0,2,1:T(8,128)(2,1)S(1)}, ...), branch_computations={%region_38.39_spmd, %region_39.40_spmd} | conditional | flops 127696896 | bytes 7292952 | solution.py:227
  95.9 2.0 %fusion.66 = f32[12,128,128]{2,1,0:T(8,128)S(1)} fusion(bf16[128,12,64]{0,2,1:T(8,128)(2,1)S(1)} %get-tuple-element.289, bf16[128,12,64]{0,2,1:T(8,128)(2,1)S(1)} %get-tuple-element.290, f32[12,128]{1,0:T(8,128)} %get-tuple-element.292, f32[12,128]{1,0:T(8,128)S(1)} %get-tuple-element.291), kind=kOutput, calls=%fused_computation.100 | convolution fusion | flops 25755648 | bytes 1191936 | tf_op jit(solution)/shard_map/cond/branch_1_fun/qhd,khd->hqk/dot_general | solution.py:38
  98.0 0.4 fusion.67
  98.5 0.4 fusion.69
  99.6 5.4 %conditional.31 = (f32[128,12,64]{0,2,1:T(8,128)S(1)}, bf16[1,128,768]{2,1,0:T(8,128)(2,1)S(1)}, bf16[1,128,768]{2,1,0:T(8,128)(2,1)}) conditional(s32[]{:T(128)} %convert_element_type.133, f32[128,12,64]{0,2,1:T(8,128)S(1)} %get-tuple-element.353, (bf16[2,128,768]{1,2,0:T(8,128)(2,1)}, bf16[128,12,64]{0,2,1:T(8,128)(2,1)S(1)}, ...), branch_computations={%region_40.41_spmd, %region_41.42_spmd} | conditional | flops 127696896 | bytes 7686168 | solution.py:227
  99.6 1.1 fusion.108
  100.7 2.0 %fusion.75 = f32[12,128,128]{2,1,0:T(8,128)S(1)} fusion(bf16[128,12,64]{0,2,1:T(8,128)(2,1)S(1)} %get-tuple-element.297, bf16[128,12,64]{0,2,1:T(8,128)(2,1)S(1)} %bitcast.294, f32[12,128]{1,0:T(8,128)} %get-tuple-element.300, f32[12,128]{1,0:T(8,128)S(1)} %get-tuple-element.299), kind=kOutput, calls=%fused_computation.114 | convolution fusion | flops 25755648 | bytes 1191936 | tf_op jit(solution)/shard_map/cond/branch_1_fun/qhd,khd->hqk/dot_general | solution.py:38
  102.7 0.4 fusion.76
  104.2 0.8 copy.130
  105.0 4.3 %conditional.32 = (f32[128,12,64]{0,2,1:T(8,128)S(1)}, bf16[1,128,768]{2,1,0:T(8,128)(2,1)}, bf16[1,128,768]{2,1,0:T(8,128)(2,1)S(1)}) conditional(s32[]{:T(128)} %convert_element_type.132, f32[128,12,64]{0,2,1:T(8,128)S(1)} %get-tuple-element.354, (bf16[2,128,768]{1,2,0:T(8,128)(2,1)S(1)}, bf16[128,12,64]{0,2,1:T(8,128)(2,1)S(1)}, ...), branch_computations={%region_42.43_spmd, %region_43.44_spmd} | conditional | flops 127696896 | bytes 7686168 | solution.py:227
  105.0 2.0 %fusion.84 = f32[12,128,128]{2,1,0:T(8,128)S(1)} fusion(bf16[128,12,64]{0,2,1:T(8,128)(2,1)S(1)} %get-tuple-element.304, bf16[128,12,64]{0,2,1:T(8,128)(2,1)S(1)} %bitcast.296, f32[12,128]{1,0:T(8,128)} %get-tuple-element.307, f32[12,128]{1,0:T(8,128)S(1)} %get-tuple-element.306), kind=kOutput, calls=%fused_computation.128 | convolution fusion | flops 25755648 | bytes 1191936 | tf_op jit(solution)/shard_map/cond/branch_1_fun/qhd,khd->hqk/dot_general | solution.py:38
  107.0 0.4 fusion.85
  108.1 0.8 copy.132
  109.3 1.8 %pad_maximum_fusion.6 = bf16[2,128,768]{2,1,0:T(8,128)(2,1)} fusion(bf16[1,128,768]{2,1,0:T(8,128)(2,1)S(1)} %get-tuple-element.486, bf16[1,128,768]{2,1,0:T(8,128)(2,1)} %get-tuple-element.485), kind=kLoop, calls=%fused_computation.161 | loop fusion | flops 196608 | bytes 786432 | tf_op jit(solution)/shard_map/stack | solution.py:234
  111.0 3.4 %collective-permute-start.7 = (bf16[2,128,768]{2,1,0:T(8,128)(2,1)}, bf16[2,128,768]{2,1,0:T(8,128)(2,1)S(1)}, u32[]{:S(2)}, u32[]{:S(2)}) collective-permute-start(bf16[2,128,768]{2,1,0:T(8,128)(2,1)} %pad_maximum_fusion.6), channel_id=1, source_target_pairs={{0,4},{2,6},{4,8},{6,10},{8,12},{10,14},{1,5},{3,7},{5,9},{7,11},{... | collective-permute-start | bytes 1179656 | tf_op jit(solution)/shard_map/ppermute | solution.py:18
  114.4 1.7 pad_maximum_fusion.5
  116.1 2.4 %collective-permute-start.6 = (bf16[2,128,768]{2,1,0:T(8,128)(2,1)}, bf16[2,128,768]{2,1,0:T(8,128)(2,1)S(1)}, u32[]{:S(2)}, u32[]{:S(2)}) collective-permute-start(bf16[2,128,768]{2,1,0:T(8,128)(2,1)} %pad_maximum_fusion.5), channel_id=1, source_target_pairs={{0,2},{2,4},{4,6},{6,8},{8,10},{10,12},{12,14},{1,3},{3,5},{5,7},{... | collective-permute-start | bytes 1179656 | tf_op jit(solution)/shard_map/ppermute | solution.py:18
  118.6 0.8 pad_maximum_fusion.3
  119.4 1.3 collective-permute-start.5
  120.7 0.8 pad_maximum_fusion.2
  121.4 1.3 collective-permute-start.4
  122.8 0.8 copy.108
  123.9 11.0 %collective-permute-done.6 = bf16[2,128,768]{2,1,0:T(8,128)(2,1)S(1)} collective-permute-done((bf16[2,128,768]{2,1,0:T(8,128)(2,1)}, bf16[2,128,768]{2,1,0:T(8,128)(2,1)S(1)}, u32[]{:S(2)}, u32[]{:S(2)}) %collective-permute-start.6) | collective-permute-done | bytes 393248 | tf_op jit(solution)/shard_map/ppermute | solution.py:18
  134.9 2.7 %collective-permute-done.4 = bf16[2,128,768]{2,1,0:T(8,128)(2,1)S(1)} collective-permute-done((bf16[2,128,768]{2,1,0:T(8,128)(2,1)}, bf16[2,128,768]{2,1,0:T(8,128)(2,1)S(1)}, u32[]{:S(2)}, u32[]{:S(2)}) %collective-permute-start.4) | collective-permute-done | bytes 393248 | tf_op jit(solution)/shard_map/ppermute | solution.py:18
  137.8 0.8 slice_bitcast_fusion
  138.6 25.5 %reduce-scatter.2.cloned.1.call-done = f32[2,32,768]{2,1,0:T(8,128)} async-done(((f32[2,256,768]{2,1,0:T(8,128)}), f32[2,32,768]{2,1,0:T(8,128)}) %reduce-scatter.2.cloned.1.call-update) | async-done | bytes 196624 | tf_op jit(solution)/shard_map/reduce_scatter | solution.py:244
  164.1 0.9 convert_element_type.150
  165.0 0.6 slice_bitcast_fusion.2
  (98 shorter events, 7.9 us)
Async XLA Ops:
  7.2 15.6 %copy-start.16 = (s32[4]{0:T(128)S(1)}, s32[4]{0:T(128)}, u32[]{:S(2)}) copy-start(s32[4]{0:T(128)} %param.45) | copy-start | bytes 52
  7.2 23.0 %copy-start.13 = (bf16[32,768]{1,0:T(8,128)(2,1)S(1)}, bf16[32,768]{1,0:T(8,128)(2,1)}, u32[]{:S(2)}) copy-start(bf16[32,768]{1,0:T(8,128)(2,1)} %param.43) | copy-start | bytes 147460
  7.2 23.0 %copy-start.14 = (bf16[32,768]{1,0:T(8,128)(2,1)S(1)}, bf16[32,768]{1,0:T(8,128)(2,1)}, u32[]{:S(2)}) copy-start(bf16[32,768]{1,0:T(8,128)(2,1)} %param.42) | copy-start | bytes 147460
  7.2 156.9 %reduce-scatter.2.cloned.1.call-start = ((), (), s32[]{:S(2)}) async-start(), calls=%async_computation.1 | async-start | bytes 1769472 | tf_op jit(solution)/shard_map/reduce_scatter | solution.py:244
  8.3 59.5 %copy-start.1 = (bf16[128,768]{0,1:T(8,128)(2,1)}, bf16[128,768]{0,1:T(8,128)(2,1)S(1)}, u32[]{:S(2)}) copy-start(bf16[128,768]{0,1:T(8,128)(2,1)S(1)} %copy.84) | copy-start | bytes 589828
  10.3 60.3 %collective-permute-start = (bf16[2,128,768]{1,2,0:T(8,128)(2,1)}, bf16[2,128,768]{1,2,0:T(8,128)(2,1)}, u32[]{:S(2)}, u32[]{:S(2)}) collective-permute-start(bf16[2,128,768]{1,2,0:T(8,128)(2,1)} %pad_maximum_fusion.1), channel_id=1, source_target_pairs={{0,4},{2,6},{4,8},{6,10},{8,12},{10,14},{1,5},{3,7},{5,9},{7,11},{... | collective-permute-start | bytes 1179656 | tf_op jit(solution)/shard_map/ppermute | solution.py:18
  16.0 54.6 %collective-permute-start.1 = (bf16[2,128,768]{1,2,0:T(8,128)(2,1)}, bf16[2,128,768]{1,2,0:T(8,128)(2,1)}, u32[]{:S(2)}, u32[]{:S(2)}) collective-permute-start(bf16[2,128,768]{1,2,0:T(8,128)(2,1)} %pad_maximum_fusion.1), channel_id=1, source_target_pairs={{0,2},{2,4},{4,6},{6,8},{8,10},{10,12},{12,14},{1,3},{3,5},{5,7},{... | collective-permute-start | bytes 1179656 | tf_op jit(solution)/shard_map/ppermute | solution.py:18
  20.1 50.5 %collective-permute-start.2 = (bf16[2,128,768]{1,2,0:T(8,128)(2,1)}, bf16[2,128,768]{1,2,0:T(8,128)(2,1)}, u32[]{:S(2)}, u32[]{:S(2)}) collective-permute-start(bf16[2,128,768]{1,2,0:T(8,128)(2,1)} %pad_maximum_fusion.1), channel_id=1, source_target_pairs={{2,0},{4,2},{6,4},{8,6},{10,8},{12,10},{14,12},{3,1},{5,3},{7,5},{... | collective-permute-start | bytes 1179656 | tf_op jit(solution)/shard_map/ppermute | solution.py:18
  21.4 52.0 %collective-permute-start.3 = (bf16[2,128,768]{1,2,0:T(8,128)(2,1)}, bf16[2,128,768]{1,2,0:T(8,128)(2,1)S(1)}, u32[]{:S(2)}, u32[]{:S(2)}) collective-permute-start(bf16[2,128,768]{1,2,0:T(8,128)(2,1)} %pad_maximum_fusion.1), channel_id=1, source_target_pairs={{4,0},{6,2},{8,4},{10,6},{12,8},{14,10},{5,1},{7,3},{9,5},{11,7},{... | collective-permute-start | bytes 1179656 | tf_op jit(solution)/shard_map/ppermute | solution.py:18
  30.2 36.6 %copy-start.10 = (bf16[128,768]{1,0:T(8,128)(2,1)S(1)}, bf16[128,768]{1,0:T(8,128)(2,1)}, u32[]{:S(2)}) copy-start(bf16[128,768]{1,0:T(8,128)(2,1)} %param.38) | copy-start | bytes 589828
  65.8 1.4 copy-start.17
  65.8 2.3 %copy-start.15 = (s32[256]{0:T(256)S(1)}, s32[256]{0:T(256)}, u32[]{:S(2)}) copy-start(s32[256]{0:T(256)} %param.47) | copy-start | bytes 3076
  65.8 3.0 %copy-start.18 = (f32[12]{0:T(128)S(1)}, f32[12]{0:T(128)}, u32[]{:S(2)}) copy-start(f32[12]{0:T(128)} %param.44) | copy-start | bytes 148
  67.1 2.3 %copy-start.6 = (bf16[1,256,768]{1,2,0:T(8,128)(2,1)}, bf16[1,256,768]{1,2,0:T(8,128)(2,1)S(1)}, u32[]{:S(2)}) copy-start(bf16[1,256,768]{1,2,0:T(8,128)(2,1)S(1)} %copy.82) | copy-start | bytes 1179652
  69.4 1.0 copy-start.11
  73.4 12.2 %copy-start.3 = (bf16[2,128,768]{1,2,0:T(8,128)(2,1)}, bf16[2,128,768]{1,2,0:T(8,128)(2,1)S(1)}, u32[]{:S(2)}) copy-start(bf16[2,128,768]{1,2,0:T(8,128)(2,1)S(1)} %collective-permute-done.3) | copy-start | bytes 1179652
  75.3 1.0 copy-start.8
  88.4 1.4 copy-start.12
  88.4 1.4 copy-start.9
  89.7 1.4 copy-start
  93.3 1.0 copy-start.7
  94.9 0.9 copy-start.2
  94.9 1.0 copy-start.5
  99.6 5.4 %copy-start.4 = (bf16[2,128,768]{1,2,0:T(8,128)(2,1)S(1)}, bf16[2,128,768]{1,2,0:T(8,128)(2,1)}, u32[]{:S(2)}) copy-start(bf16[2,128,768]{1,2,0:T(8,128)(2,1)} %copy-done.3) | copy-start | bytes 1179652
  111.0 12.8 %collective-permute-start.7 = (bf16[2,128,768]{2,1,0:T(8,128)(2,1)}, bf16[2,128,768]{2,1,0:T(8,128)(2,1)S(1)}, u32[]{:S(2)}, u32[]{:S(2)}) collective-permute-start(bf16[2,128,768]{2,1,0:T(8,128)(2,1)} %pad_maximum_fusion.6), channel_id=1, source_target_pairs={{0,4},{2,6},{4,8},{6,10},{8,12},{10,14},{1,5},{3,7},{5,9},{7,11},{... | collective-permute-start | bytes 1179656 | tf_op jit(solution)/shard_map/ppermute | solution.py:18
  116.1 18.7 %collective-permute-start.6 = (bf16[2,128,768]{2,1,0:T(8,128)(2,1)}, bf16[2,128,768]{2,1,0:T(8,128)(2,1)S(1)}, u32[]{:S(2)}, u32[]{:S(2)}) collective-permute-start(bf16[2,128,768]{2,1,0:T(8,128)(2,1)} %pad_maximum_fusion.5), channel_id=1, source_target_pairs={{0,2},{2,4},{4,6},{6,8},{8,10},{10,12},{12,14},{1,3},{3,5},{5,7},{... | collective-permute-start | bytes 1179656 | tf_op jit(solution)/shard_map/ppermute | solution.py:18
  119.4 15.5 %collective-permute-start.5 = (bf16[2,128,768]{2,1,0:T(8,128)(2,1)}, bf16[2,128,768]{2,1,0:T(8,128)(2,1)S(1)}, u32[]{:S(2)}, u32[]{:S(2)}) collective-permute-start(bf16[2,128,768]{2,1,0:T(8,128)(2,1)} %pad_maximum_fusion.3), channel_id=1, source_target_pairs={{2,0},{4,2},{6,4},{8,6},{10,8},{12,10},{14,12},{3,1},{5,3},{7,5},{... | collective-permute-start | bytes 1179656 | tf_op jit(solution)/shard_map/ppermute | solution.py:18
  121.4 16.2 %collective-permute-start.4 = (bf16[2,128,768]{2,1,0:T(8,128)(2,1)}, bf16[2,128,768]{2,1,0:T(8,128)(2,1)S(1)}, u32[]{:S(2)}, u32[]{:S(2)}) collective-permute-start(bf16[2,128,768]{2,1,0:T(8,128)(2,1)} %pad_maximum_fusion.2), channel_id=1, source_target_pairs={{4,0},{6,2},{8,4},{10,6},{12,8},{14,10},{5,1},{7,3},{9,5},{11,7},{... | collective-permute-start | bytes 1179656 | tf_op jit(solution)/shard_map/ppermute | solution.py:18
Sparse Core Ops, SparseCore 0:
  93.5 70.5 reduce-scatter.1
where the time goes:
time: 175 us; the launch traced here: 173 us
  waiting for transfers between devices  39.5 us (23%)
  blocking collectives  35.6 us (20%)
  between operations  21.1 us (12%)
  starting transfers between devices  20.8 us (12%)
  local copies, waits for them, and re-layouts  20.5 us (12%)
  matrix products  20.3 us (12%)
  other arithmetic  14.3 us (8%)
    all_gather x1, blocking collectives, shards(): lax.all_gather(jnp.stack([ctrl_key, ctrl_value]), 'seq', axis=1, tiled=True)  35.6 us
    reduce_scatter x1, waiting for transfers between devices, shards(): lax.psum_scatter(ctrl_terms, 'seq', scatter_dimension=1, tiled=True)  25.5 us
    ppermute x8, starting transfers between devices, passed_along(): return lax.ppermute(block, axis, route)  20.7 us
    ppermute x8, waiting for transfers between devices, passed_along(): return lax.ppermute(block, axis, route)  14 us
    dot_general x7, matrix products, scores_of(): jnp.einsum('qhd,khd->hqk', q_blk, k_blk, preferred_element_type=jnp.float32)  7.5 us
    dot_general x3, matrix products, add_values(): jnp.einsum('hqk,khd->qhd', weights, v_blk, preferred_element_type=jnp.flo...  5.48 us
    unnamed x43, local copies, waits for them, and re-layouts  5.38 us
    another operation x5, other arithmetic, shards(): slot_pieces = jnp.stack([key_grad, value_grad]).reshape(2, BLK, width_all)  5.1 us
  transfers between devices with their start and end apart: 9, of which 4 were waited for; matrix products, arithmetic and copies ran while one was open for 17% of the time, Pallas kernels for 0%

commit v1 on v0

--- a/solution.py
+++ b/solution.py
@@ -3,6 +3,8 @@
 import jax
 import jax.numpy as jnp
 from jax import lax
+from jax.experimental import pallas as pl
+from jax.experimental.pallas import tpu as pltpu
 from jax.sharding import PartitionSpec as P
 
 BLK = 128
@@ -249,9 +251,299 @@
     return (attended, d_query, key_results[0], key_results[1], ctrl_results[0], ctrl_results[1])
 
 
+MESH = pl.DeviceIdType.MESH
+SLOTS = (-2, -1, 1, 2)
+LANES = 128
+
+
+def masked_pair(rows, low_lanes, factor):
+    first = low_lanes.astype(jnp.float32) * factor
+    second = factor - first
+    return jnp.concatenate(
+        [rows * first.astype(rows.dtype), rows * second.astype(rows.dtype)], axis=0
+    )
+
+
+def dot(left, right, left_dim, right_dim):
+    return lax.dot_general(
+        left, right, (((left_dim,), (right_dim,)), ((), ())), preferred_element_type=jnp.float32
+    )
+
+
+def tube_kernel(
+    count, q_ref, k_ref, v_ref, g_ref, ck_ref, cv_ref, bias_ref, flag_ref,
+    att_ref, dq_ref, dk_ref, dv_ref, dck_ref, dcv_ref,
+    own, window, ctrl, own_grad, grad_out, grad_in, ctrl_out, ctrl_in,
+    kv_send, kv_recv, ctrl_send, ctrl_recv, grad_send, grad_recv, sum_send, sum_recv,
+):
+    me = lax.axis_index("seq")
+    rows = q_ref.shape[0]
+    ctrl_rows = ck_ref.shape[0]
+    pairs = q_ref.shape[1] // LANES
+    low_lanes = lax.broadcasted_iota(jnp.int32, (1, LANES), 1) < LANES // 2
+
+    def inside(device):
+        return (device >= 0) & (device < count)
+
+    def columns(pair):
+        return pl.ds(pl.multiple_of(pair * LANES, LANES), LANES)
+
+    def kv_copy(pair, slot):
+        return pltpu.make_async_remote_copy(
+            own.at[pair], window.at[pair, slot], kv_send.at[pair, slot], kv_recv.at[pair, slot],
+            device_id={"seq": me - SLOTS[slot]}, device_id_type=MESH,
+        )
+
+    def grad_copy(pair, slot):
+        return pltpu.make_async_remote_copy(
+            grad_out.at[pair, slot], grad_in.at[pair, slot],
+            grad_send.at[pair, slot], grad_recv.at[pair, slot],
+            device_id={"seq": me + SLOTS[slot]}, device_id_type=MESH,
+        )
+
+    def ctrl_copy(pair, step):
+        return pltpu.make_async_remote_copy(
+            ctrl.at[pair, me], ctrl.at[pair, me], ctrl_send.at[pair, step], ctrl_recv.at[pair, step],
+            device_id={"seq": lax.rem(me + step, count)}, device_id_type=MESH,
+        )
+
+    def ctrl_arrival(pair, step):
+        source = lax.rem(me - step + count, count)
+        return pltpu.make_async_remote_copy(
+            ctrl.at[pair, source], ctrl.at[pair, source],
+            ctrl_send.at[pair, step], ctrl_recv.at[pair, step],
+            device_id={"seq": source}, device_id_type=MESH,
+        )
+
+    def sum_copy(pair, step):
+        target = lax.rem(me + step, count)
+        return pltpu.make_async_remote_copy(
+            ctrl_out.at[pair, target], ctrl_in.at[pair, me],
+            sum_send.at[pair, step], sum_recv.at[pair, step],
+            device_id={"seq": target}, device_id_type=MESH,
+        )
+
+    def sum_arrival(pair, step):
+        source = lax.rem(me - step + count, count)
+        return pltpu.make_async_remote_copy(
+            ctrl_out.at[pair, source], ctrl_in.at[pair, source],
+            sum_send.at[pair, step], sum_recv.at[pair, step],
+            device_id={"seq": source}, device_id_type=MESH,
+        )
+
+    def pack(pair, _):
+        own[pair, 0] = k_ref[:, columns(pair)]
+        own[pair, 1] = v_ref[:, columns(pair)]
+        ctrl[pair, me, 0] = ck_ref[:, columns(pair)]
+        ctrl[pair, me, 1] = cv_ref[:, columns(pair)]
+        return 0
+
+    lax.fori_loop(0, pairs, pack, 0)
+    for slot, distance in enumerate(SLOTS):
+        @pl.when(jnp.logical_not(inside(me + distance)))
+        def _():
+            window[:, slot] = jnp.zeros((pairs,) + window.shape[2:], window.dtype)
+
+        @pl.when(jnp.logical_not(inside(me - distance)))
+        def _():
+            grad_in[:, slot] = jnp.zeros((pairs,) + grad_in.shape[2:], grad_in.dtype)
+
+    barrier = pltpu.get_barrier_semaphore()
+    for step in range(1, count):
+        pl.semaphore_signal(
+            barrier, inc=1, device_id={"seq": lax.rem(me + step, count)}, device_id_type=MESH
+        )
+    pl.semaphore_wait(barrier, count - 1)
+
+    def send(pair, _):
+        for step in range(1, count):
+            ctrl_copy(pair, step).start()
+        for slot, distance in enumerate(SLOTS):
+            @pl.when(inside(me - distance))
+            def _():
+                kv_copy(pair, slot).start()
+        return 0
+
+    lax.fori_loop(0, pairs, send, 0)
+
+    lower, lower2, upper, upper2 = (flag_ref[i] > 0 for i in (1, 0, 2, 3))
+    zero_block = jnp.zeros((rows, LANES), jnp.bfloat16)
+    zero_grad = jnp.zeros((rows, LANES), jnp.float32)
+
+    def work(pair, _):
+        for step in range(1, count):
+            ctrl_arrival(pair, step).wait_recv()
+        for slot, distance in enumerate(SLOTS):
+            @pl.when(inside(me + distance))
+            def _():
+                kv_copy(pair, slot).wait_recv()
+
+        def gathered(kind):
+            first = jnp.where(
+                lower, window[pair, 1, kind], jnp.where(upper2, window[pair, 3, kind], zero_block)
+            )
+            second = jnp.where(
+                upper, window[pair, 2, kind], jnp.where(lower2, window[pair, 0, kind], zero_block)
+            )
+            shared = ctrl[pair, :, kind].reshape(count * ctrl_rows, LANES)
+            return jnp.concatenate([first, own[pair, kind], second, shared], axis=0)
+
+        keys = gathered(0)
+        values = gathered(1)
+        q_two = masked_pair(q_ref[:, columns(pair)], low_lanes, 0.125)
+        g_two = masked_pair(g_ref[:, columns(pair)], low_lanes, 1.0)
+        scores = dot(q_two, keys, 1, 1)
+        bias = bias_ref[pair]
+        scores = jnp.concatenate(
+            [scores[:rows] + bias[0:1], scores[rows:] + bias[1:2]], axis=0
+        )
+        raised = jnp.exp(scores - jnp.max(scores, axis=1, keepdims=True))
+        weights = raised * (1.0 / jnp.sum(raised, axis=1, keepdims=True))
+        rounded = weights.astype(jnp.bfloat16)
+        out_two = dot(rounded, values, 1, 0)
+        attended = jnp.where(low_lanes, out_two[:rows], out_two[rows:]).astype(jnp.bfloat16)
+        att_ref[:, columns(pair)] = attended
+        attended = attended.astype(jnp.float32)
+        delta = jnp.sum(
+            g_two.astype(jnp.float32) * jnp.concatenate([attended, attended], axis=0),
+            axis=1, keepdims=True,
+        )
+        d_scores = (weights * (dot(g_two, values, 1, 1) - delta)).astype(jnp.bfloat16)
+        dq_two = dot(d_scores, keys, 1, 0) * 0.125
+        dq_ref[:, columns(pair)] = jnp.where(low_lanes, dq_two[:rows], dq_two[rows:]).astype(
+            jnp.bfloat16
+        )
+        for kind, grads in enumerate((dot(d_scores, q_two, 0, 0), dot(rounded, g_two, 0, 0))):
+            first, second = grads[:rows], grads[2 * rows : 3 * rows]
+            own_grad[pair, kind] = grads[rows : 2 * rows].astype(jnp.bfloat16)
+            for slot, (chosen, term) in enumerate(
+                ((lower2, second), (lower, first), (upper, second), (upper2, first))
+            ):
+                grad_out[pair, slot, kind] = jnp.where(chosen, term, zero_grad).astype(jnp.bfloat16)
+            ctrl_out[pair, :, kind] = (
+                grads[3 * rows :].astype(jnp.bfloat16).reshape(count, ctrl_rows, LANES)
+            )
+        for step in range(1, count):
+            sum_copy(pair, step).start()
+        for slot, distance in enumerate(SLOTS):
+            @pl.when(inside(me + distance))
+            def _():
+                grad_copy(pair, slot).start()
+        return 0
+
+    lax.fori_loop(0, pairs, work, 0)
+
+    def finish(pair, _):
+        ctrl_in[pair, me] = ctrl_out[pair, me]
+        for step in range(1, count):
+            sum_arrival(pair, step).wait_recv()
+        for slot, distance in enumerate(SLOTS):
+            @pl.when(inside(me - distance))
+            def _():
+                grad_copy(pair, slot).wait_recv()
+        for kind, (key_ref, ctrl_ref) in enumerate(((dk_ref, dck_ref), (dv_ref, dcv_ref))):
+            total = own_grad[pair, kind].astype(jnp.float32)
+            for slot in range(len(SLOTS)):
+                total += grad_in[pair, slot, kind].astype(jnp.float32)
+            key_ref[:, columns(pair)] = total.astype(jnp.bfloat16)
+            ctrl_total = ctrl_in[pair, 0, kind].astype(jnp.float32)
+            for source in range(1, count):
+                ctrl_total += ctrl_in[pair, source, kind].astype(jnp.float32)
+            ctrl_ref[:, columns(pair)] = ctrl_total.astype(jnp.bfloat16)
+        return 0
+
+    lax.fori_loop(0, pairs, finish, 0)
+
+    def drain(pair, _):
+        for step in range(1, count):
+            ctrl_copy(pair, step).wait_send()
+            sum_copy(pair, step).wait_send()
+        for slot, distance in enumerate(SLOTS):
+            @pl.when(inside(me - distance))
+            def _():
+                kv_copy(pair, slot).wait_send()
+
+            @pl.when(inside(me + distance))
+            def _():
+                grad_copy(pair, slot).wait_send()
+        return 0
+
+    lax.fori_loop(0, pairs, drain, 0)
+
+
+def fused_shards(
+    query_states, key_states, value_states, d_attended, ctrl_key, ctrl_value,
+    ctrl_bias, tube_lengths, tube_owner, ctrl_owner,
+):
+    count = lax.axis_size("seq")
+    rows, width = query_states.shape
+    ctrl_rows = ctrl_key.shape[0]
+    pairs = width // LANES
+    tube_index, owner_index = tube_tables(tube_lengths, tube_owner, count)
+    position = lax.axis_index("seq")
+    mine = tube_index[position]
+
+    def member(distance):
+        block = position + distance
+        return (block >= 0) & (block < count) & (tube_index[jnp.clip(block, 0, count - 1)] == mine)
+
+    flags = jnp.stack([member(distance) for distance in SLOTS])
+    blocks_open = jnp.stack([flags[1] | flags[3], True, flags[2] | flags[0]])
+    tube_bias = jnp.where(jnp.repeat(blocks_open, rows), 0.0, MASKED)
+    heads = ctrl_bias.shape[0]
+    ctrl_part = jnp.where(
+        (ctrl_owner == owner_index[position])[None, :], ctrl_bias[:, None], MASKED
+    )
+    bias = jnp.concatenate(
+        [jnp.broadcast_to(tube_bias[None, :], (heads, 3 * rows)), ctrl_part], axis=1
+    ).reshape(pairs, 2, -1)
+    vmem = pl.BlockSpec(memory_space=pltpu.VMEM)
+    block = jax.ShapeDtypeStruct((rows, width), jnp.bfloat16)
+    ctrl_block = jax.ShapeDtypeStruct((ctrl_rows, width), jnp.bfloat16)
+    tile = (2, rows, LANES)
+    ctrl_tile = (count, 2, ctrl_rows, LANES)
+    slots = len(SLOTS)
+    return pl.pallas_call(
+        partial(tube_kernel, count),
+        out_shape=(block, block, block, block, ctrl_block, ctrl_block),
+        in_specs=[vmem] * 7 + [pl.BlockSpec(memory_space=pltpu.SMEM)],
+        out_specs=[vmem] * 6,
+        scratch_shapes=[
+            pltpu.VMEM((pairs,) + tile, jnp.bfloat16),
+            pltpu.VMEM((pairs, slots) + tile, jnp.bfloat16),
+            pltpu.VMEM((pairs,) + ctrl_tile, jnp.bfloat16),
+            pltpu.VMEM((pairs,) + tile, jnp.bfloat16),
+            pltpu.VMEM((pairs, slots) + tile, jnp.bfloat16),
+            pltpu.VMEM((pairs, slots) + tile, jnp.bfloat16),
+            pltpu.VMEM((pairs,) + ctrl_tile, jnp.bfloat16),
+            pltpu.VMEM((pairs,) + ctrl_tile, jnp.bfloat16),
+            pltpu.SemaphoreType.DMA((pairs, slots)),
+            pltpu.SemaphoreType.DMA((pairs, slots)),
+            pltpu.SemaphoreType.DMA((pairs, count)),
+            pltpu.SemaphoreType.DMA((pairs, count)),
+            pltpu.SemaphoreType.DMA((pairs, slots)),
+            pltpu.SemaphoreType.DMA((pairs, slots)),
+            pltpu.SemaphoreType.DMA((pairs, count)),
+            pltpu.SemaphoreType.DMA((pairs, count)),
+        ],
+        compiler_params=pltpu.CompilerParams(
+            collective_id=0, has_side_effects=True, vmem_limit_bytes=48 * 1024 * 1024
+        ),
+    )(
+        query_states, key_states, value_states, d_attended, ctrl_key, ctrl_value,
+        bias, flags.astype(jnp.int32),
+    )
+
+
+def fused_or_plain(*arrays):
+    tile_rows = 16
+    fits = arrays[4].shape[0] % tile_rows == 0 and arrays[0].shape[0] == BLK
+    return (fused_shards if fits else shards)(*arrays)
+
+
 def solution(mesh):
     return jax.shard_map(
-        shards,
+        fused_or_plain,
         mesh=mesh,
         in_specs=(
             P(("groups", "seq"), "head"),

time: 175 us -> 95.6 us (0.55)
  Pallas kernels: 0 us -> 74.7 us
  waiting for transfers between devices: 39.5 us -> 0 us
  blocking collectives: 35.6 us -> 0 us
  starting transfers between devices: 20.8 us -> 0 us
  matrix products: 20.3 us -> 0 us
  between operations: 21.1 us -> 5.93 us
  other arithmetic: 14.3 us -> 3.28 us
  local copies, waits for them, and re-layouts: 20.5 us -> 10.3 us
    pallas_call x0 -> x1, Pallas kernels: none -> 74.7 us  [fused_shards(): pl.pallas_call(partial(tube_kernel, count), out_shape=(block, block, bloc...]
    all_gather x1 -> x0, blocking collectives: 35.6 us -> none  [shards(): lax.all_gather(jnp.stack([ctrl_key, ctrl_value]), 'seq', axis=1, tiled=True)]
    reduce_scatter x1 -> x0, waiting for transfers between devices: 25.5 us -> none  [shards(): lax.psum_scatter(ctrl_terms, 'seq', scatter_dimension=1, tiled=True)]
    ppermute x8 -> x0, starting transfers between devices: 20.7 us -> none  [passed_along(): return lax.ppermute(block, axis, route)]
    dot_general x27 -> x0, matrix products: 20.3 us -> none  [the longest x7 7.5 us: scores_of(): jnp.einsum('qhd,khd->hqk', q_blk, k_blk, preferred_element_type=jnp.float32)]
    ppermute x8 -> x0, waiting for transfers between devices: 14 us -> none  [passed_along(): return lax.ppermute(block, axis, route)]
    another operation x9 -> x1, other arithmetic: 7.36 us -> 0.88 us  [the longest x5 5.1 us: shards(): slot_pieces = jnp.stack([key_grad, value_grad]).reshape(2, BLK, width_all)]
    slice x9 -> x0, local copies, waits for them, and re-layouts: 5.8 us -> none  [the longest x6 4.64 us: window_block(): window[slot_index][member_index, block_local * BLK:(block_local + 1) * BLK]]
  transfers between devices with their start and end apart: 9 -> 0, of which waited for: 4 -> 0; matrix products, arithmetic and copies ran while one was open for 17% -> 0% of each run, Pallas kernels for 0% -> 0%
where the time goes in v1:
time: 95.6 us; the launch traced here: 94.2 us
  Pallas kernels  74.7 us (78%)
  local copies, waits for them, and re-layouts  10.3 us (11%)
  between operations  5.93 us (6%)
  other arithmetic  3.28 us (3%)
    pallas_call x1, Pallas kernels, fused_shards(): pl.pallas_call(partial(tube_kernel, count), out_shape=(block, block, bloc...  74.7 us
    unnamed x18, local copies, waits for them, and re-layouts  8.32 us

profile of v1, /device:TPU:0, one launch (start us, length us, event | category | flops | bytes accessed | tf_op | source)
XLA Modules:
  0.0 94.2 jit_solution(460453550517517445)
XLA Ops:
  0.6 0.0 copy-start
  0.7 0.9 reduce-window.8
  1.6 0.1 convert_reduce_fusion
  1.6 0.7 select_reduce_fusion
  2.4 0.6 dynamic_slice.23
  3.0 0.6 fusion
  8.8 0.1 add_select_fusion
  8.9 0.1 add_convert_fusion.flag_ref
  8.9 1.3 %broadcast_compare_fusion = pred[256]{0:T(512)(128)(4,1)S(1)} fusion(s32[256]{0:T(256)} %param.19, s32[]{:T(128)} %bitcast.9), kind=kLoop, calls=%fused_computation.9 | loop fusion | flops 256 | bytes 1284 | tf_op jit(solution)/shard_map/eq | solution.py:495
  10.3 0.1 broadcast_bitcast_fusion
  10.3 0.7 broadcast_in_dim.65
  11.1 0.1 broadcast_select_fusion
  11.2 0.0 copy-done
  11.2 0.0 copy-start.1
  11.2 0.9 copy-done.1
  12.1 0.0 copy-start.2
  12.1 0.9 copy-done.2
  13.0 0.0 copy-start.3
  13.0 0.9 copy-done.3
  14.0 0.0 copy-start.4
  14.0 0.8 copy-done.4
  14.8 0.0 copy-start.5
  14.8 0.8 copy-done.5
  15.6 74.7 %shard_map.145 = (bf16[128,768]{1,0:T(8,128)(2,1)S(1)}, bf16[128,768]{1,0:T(8,128)(2,1)S(1)}, bf16[128,768]{1,0:T(8,128)(2,1)S(1)}, bf16[128,768]{1,0:T(8,128)(2...) custom-call(bf16[128,768]{1,0:T(8,128)(2,1)S(1)} %copy-done, bf16[128,768]{1,0:T(8,128)(2,1)S(1)} %copy-done.1, ...), custom_call_target="tpu_custom_call" | custom-call | tf_op jit(solution)/shard_map/pallas_call | solution.py:506
  90.3 0.7 copy.22
  91.0 0.7 copy.23
  91.6 0.7 copy.24
  92.3 0.7 copy.25
  93.0 0.6 copy.26
  93.6 0.6 copy.27
  (2 shorter events, 0.0 us)
Async XLA Ops:
  0.6 10.5 %copy-start = (bf16[128,768]{1,0:T(8,128)(2,1)S(1)}, bf16[128,768]{1,0:T(8,128)(2,1)}, u32[]{:S(2)}) copy-start(bf16[128,768]{1,0:T(8,128)(2,1)} %q_ref.1) | copy-start | bytes 589828
  11.2 0.9 copy-start.1
  12.1 0.9 copy-start.2
  13.0 0.9 copy-start.3
  14.0 0.8 copy-start.4
  14.8 0.8 copy-start.5

commit v2 on v1

--- a/solution.py
+++ b/solution.py
@@ -254,6 +254,7 @@
 MESH = pl.DeviceIdType.MESH
 SLOTS = (-2, -1, 1, 2)
 LANES = 128
+AHEAD = 2
 
 
 def masked_pair(rows, low_lanes, factor):
@@ -271,14 +272,21 @@
 
 
 def tube_kernel(
-    count, q_ref, k_ref, v_ref, g_ref, ck_ref, cv_ref, bias_ref, flag_ref,
+    count, q_hbm, k_hbm, v_hbm, g_hbm, ck_hbm, cv_hbm,
+    bias_hbm, length_hbm, owner_hbm, tag_hbm,
     att_ref, dq_ref, dk_ref, dv_ref, dck_ref, dcv_ref,
-    own, window, ctrl, own_grad, grad_out, grad_in, ctrl_out, ctrl_in,
-    kv_send, kv_recv, ctrl_send, ctrl_recv, grad_send, grad_recv, sum_send, sum_recv,
+    q_ref, g_ref, own, window, ctrl, own_grad, grad_out, grad_in, ctrl_out, ctrl_mid, ctrl_in,
+    bias_ref, length_ref, owner_ref, tag_ref, load_sem, query_sem,
+    kv_send, kv_recv, ctrl_send, ctrl_recv, grad_send, grad_recv,
+    mid_send, mid_recv, sum_send, sum_recv,
 ):
     me = lax.axis_index("seq")
+    column = lax.rem(me, 2)
+    peer = me + 1 - 2 * column
+    level = me // 2
+    levels = count // 2
     rows = q_ref.shape[0]
-    ctrl_rows = ck_ref.shape[0]
+    ctrl_rows = ck_hbm.shape[0]
     pairs = q_ref.shape[1] // LANES
     low_lanes = lax.broadcasted_iota(jnp.int32, (1, LANES), 1) < LANES // 2
 
@@ -301,44 +309,91 @@
             device_id={"seq": me + SLOTS[slot]}, device_id_type=MESH,
         )
 
+    def mate(step):
+        return lax.rem(me + 2 * step, count)
+
+    def mate_before(step):
+        return lax.rem(me - 2 * step + count, count)
+
     def ctrl_copy(pair, step):
         return pltpu.make_async_remote_copy(
             ctrl.at[pair, me], ctrl.at[pair, me], ctrl_send.at[pair, step], ctrl_recv.at[pair, step],
-            device_id={"seq": lax.rem(me + step, count)}, device_id_type=MESH,
+            device_id={"seq": mate(step) if step else peer}, device_id_type=MESH,
         )
 
     def ctrl_arrival(pair, step):
-        source = lax.rem(me - step + count, count)
+        source = mate_before(step) if step else peer
         return pltpu.make_async_remote_copy(
             ctrl.at[pair, source], ctrl.at[pair, source],
             ctrl_send.at[pair, step], ctrl_recv.at[pair, step],
             device_id={"seq": source}, device_id_type=MESH,
         )
 
+    def ctrl_onward(pair, step):
+        source = mate_before(step)
+        return pltpu.make_async_remote_copy(
+            ctrl.at[pair, source], ctrl.at[pair, source],
+            ctrl_send.at[pair, levels + step], ctrl_recv.at[pair, levels + step],
+            device_id={"seq": peer}, device_id_type=MESH,
+        )
+
+    def ctrl_onward_arrival(pair, step):
+        source = mate_before(step) + 1 - 2 * column
+        return pltpu.make_async_remote_copy(
+            ctrl.at[pair, source], ctrl.at[pair, source],
+            ctrl_send.at[pair, levels + step], ctrl_recv.at[pair, levels + step],
+            device_id={"seq": peer}, device_id_type=MESH,
+        )
+
+    def mid_copy(pair):
+        return pltpu.make_async_remote_copy(
+            ctrl_out.at[pair, 1 - column], ctrl_mid.at[pair], mid_send.at[pair], mid_recv.at[pair],
+            device_id={"seq": peer}, device_id_type=MESH,
+        )
+
     def sum_copy(pair, step):
-        target = lax.rem(me + step, count)
-        return pltpu.make_async_remote_copy(
-            ctrl_out.at[pair, target], ctrl_in.at[pair, me],
+        return pltpu.make_async_remote_copy(
+            ctrl_out.at[pair, column, mate(step) // 2], ctrl_in.at[pair, level],
             sum_send.at[pair, step], sum_recv.at[pair, step],
-            device_id={"seq": target}, device_id_type=MESH,
+            device_id={"seq": mate(step)}, device_id_type=MESH,
         )
 
     def sum_arrival(pair, step):
-        source = lax.rem(me - step + count, count)
-        return pltpu.make_async_remote_copy(
-            ctrl_out.at[pair, source], ctrl_in.at[pair, source],
+        source = mate_before(step)
+        return pltpu.make_async_remote_copy(
+            ctrl_out.at[pair, column, level], ctrl_in.at[pair, source // 2],
             sum_send.at[pair, step], sum_recv.at[pair, step],
             device_id={"seq": source}, device_id_type=MESH,
         )
 
-    def pack(pair, _):
-        own[pair, 0] = k_ref[:, columns(pair)]
-        own[pair, 1] = v_ref[:, columns(pair)]
-        ctrl[pair, me, 0] = ck_ref[:, columns(pair)]
-        ctrl[pair, me, 1] = cv_ref[:, columns(pair)]
+    def loads(pair):
+        part = columns(pair)
+        return [
+            pltpu.make_async_copy(source.at[:, part], target, load_sem.at[pair, i])
+            for i, (source, target) in enumerate((
+                (ck_hbm, ctrl.at[pair, me, 0]), (cv_hbm, ctrl.at[pair, me, 1]),
+                (k_hbm, own.at[pair, 0]), (v_hbm, own.at[pair, 1]),
+            ))
+        ]
+
+    def query_loads():
+        return (
+            pltpu.make_async_copy(q_hbm, q_ref, query_sem.at[0]),
+            pltpu.make_async_copy(g_hbm, g_ref, query_sem.at[1]),
+            pltpu.make_async_copy(bias_hbm, bias_ref, query_sem.at[2]),
+            pltpu.make_async_copy(length_hbm, length_ref, query_sem.at[3]),
+            pltpu.make_async_copy(owner_hbm, owner_ref, query_sem.at[4]),
+            pltpu.make_async_copy(tag_hbm, tag_ref, query_sem.at[5]),
+        )
+
+    def start_loads(pair, _):
+        for copy in loads(pair):
+            copy.start()
         return 0
 
-    lax.fori_loop(0, pairs, pack, 0)
+    lax.fori_loop(0, pairs, start_loads, 0)
+    for copy in query_loads():
+        copy.start()
     for slot, distance in enumerate(SLOTS):
         @pl.when(jnp.logical_not(inside(me + distance)))
         def _():
@@ -356,7 +411,9 @@
     pl.semaphore_wait(barrier, count - 1)
 
     def send(pair, _):
-        for step in range(1, count):
+        for copy in loads(pair):
+            copy.wait()
+        for step in range(levels):
             ctrl_copy(pair, step).start()
         for slot, distance in enumerate(SLOTS):
             @pl.when(inside(me - distance))
@@ -366,13 +423,54 @@
 
     lax.fori_loop(0, pairs, send, 0)
 
-    lower, lower2, upper, upper2 = (flag_ref[i] > 0 for i in (1, 0, 2, 3))
+    for copy in query_loads():
+        copy.wait()
+    tubes = length_ref.shape[0]
+    ends = []
+    for tube in range(tubes):
+        ends.append(length_ref[tube] + (ends[-1] if ends else 0))
+
+    def tube_at(block):
+        return sum(jnp.where(end <= block, 1, 0) for end in ends)
+
+    mine = tube_at(me)
+    owner = sum(jnp.where(mine == tube, owner_ref[tube], 0) for tube in range(tubes))
+    lower2, lower, upper, upper2 = (
+        inside(me + distance) & (tube_at(me + distance) == mine) for distance in SLOTS
+    )
+    first_bias = jnp.full((1, rows), jnp.where(lower | upper2, 0.0, MASKED), jnp.float32)
+    second_bias = jnp.full((1, rows), jnp.where(upper | lower2, 0.0, MASKED), jnp.float32)
+    own_bias = jnp.zeros((1, rows), jnp.float32)
+    ctrl_open = tag_ref[...].reshape(1, count * ctrl_rows) == owner
+
+    def bias_of(head):
+        ctrl_bias = jnp.where(ctrl_open, bias_ref[head], MASKED)
+        return jnp.concatenate([first_bias, own_bias, second_bias, ctrl_bias], axis=1)
+
     zero_block = jnp.zeros((rows, LANES), jnp.bfloat16)
     zero_grad = jnp.zeros((rows, LANES), jnp.float32)
 
+    def relay(pair):
+        for step in range(1, levels):
+            ctrl_arrival(pair, step).wait_recv()
+            ctrl_onward(pair, step).start()
+
+    def column_sums(pair):
+        mid_copy(pair).wait()
+        ctrl_out[pair, column] = (
+            ctrl_out[pair, column].astype(jnp.float32) + ctrl_mid[pair].astype(jnp.float32)
+        ).astype(jnp.bfloat16)
+        for step in range(1, levels):
+            sum_copy(pair, step).start()
+
     def work(pair, _):
-        for step in range(1, count):
-            ctrl_arrival(pair, step).wait_recv()
+        @pl.when(pair + AHEAD < pairs)
+        def _():
+            relay(pair + AHEAD)
+
+        ctrl_arrival(pair, 0).wait_recv()
+        for step in range(1, levels):
+            ctrl_onward_arrival(pair, step).wait_recv()
         for slot, distance in enumerate(SLOTS):
             @pl.when(inside(me + distance))
             def _():
@@ -393,9 +491,8 @@
         q_two = masked_pair(q_ref[:, columns(pair)], low_lanes, 0.125)
         g_two = masked_pair(g_ref[:, columns(pair)], low_lanes, 1.0)
         scores = dot(q_two, keys, 1, 1)
-        bias = bias_ref[pair]
         scores = jnp.concatenate(
-            [scores[:rows] + bias[0:1], scores[rows:] + bias[1:2]], axis=0
+            [scores[:rows] + bias_of(2 * pair), scores[rows:] + bias_of(2 * pair + 1)], axis=0
         )
         raised = jnp.exp(scores - jnp.max(scores, axis=1, keepdims=True))
         weights = raised * (1.0 / jnp.sum(raised, axis=1, keepdims=True))
@@ -420,22 +517,31 @@
                 ((lower2, second), (lower, first), (upper, second), (upper2, first))
             ):
                 grad_out[pair, slot, kind] = jnp.where(chosen, term, zero_grad).astype(jnp.bfloat16)
-            ctrl_out[pair, :, kind] = (
-                grads[3 * rows :].astype(jnp.bfloat16).reshape(count, ctrl_rows, LANES)
-            )
-        for step in range(1, count):
-            sum_copy(pair, step).start()
+            shared = grads[3 * rows :].astype(jnp.bfloat16)
+            for device in range(count):
+                ctrl_out[pair, device % 2, device // 2, kind] = (
+                    shared[device * ctrl_rows : (device + 1) * ctrl_rows]
+                )
+        mid_copy(pair).start()
         for slot, distance in enumerate(SLOTS):
             @pl.when(inside(me + distance))
             def _():
                 grad_copy(pair, slot).start()
+
+        @pl.when(pair > 0)
+        def _():
+            column_sums(pair - 1)
+
         return 0
 
+    for pair in range(AHEAD):
+        relay(pair)
     lax.fori_loop(0, pairs, work, 0)
+    column_sums(pairs - 1)
 
     def finish(pair, _):
-        ctrl_in[pair, me] = ctrl_out[pair, me]
-        for step in range(1, count):
+        ctrl_in[pair, level] = ctrl_out[pair, column, level]
+        for step in range(1, levels):
             sum_arrival(pair, step).wait_recv()
         for slot, distance in enumerate(SLOTS):
             @pl.when(inside(me - distance))
@@ -447,7 +553,7 @@
                 total += grad_in[pair, slot, kind].astype(jnp.float32)
             key_ref[:, columns(pair)] = total.astype(jnp.bfloat16)
             ctrl_total = ctrl_in[pair, 0, kind].astype(jnp.float32)
-            for source in range(1, count):
+            for source in range(1, levels):
                 ctrl_total += ctrl_in[pair, source, kind].astype(jnp.float32)
             ctrl_ref[:, columns(pair)] = ctrl_total.astype(jnp.bfloat16)
         return 0
@@ -455,8 +561,10 @@
     lax.fori_loop(0, pairs, finish, 0)
 
     def drain(pair, _):
-        for step in range(1, count):
+        for step in range(levels):
             ctrl_copy(pair, step).wait_send()
+        for step in range(1, levels):
+            ctrl_onward(pair, step).wait_send()
             sum_copy(pair, step).wait_send()
         for slot, distance in enumerate(SLOTS):
             @pl.when(inside(me - distance))
@@ -479,60 +587,73 @@
     rows, width = query_states.shape
     ctrl_rows = ctrl_key.shape[0]
     pairs = width // LANES
-    tube_index, owner_index = tube_tables(tube_lengths, tube_owner, count)
-    position = lax.axis_index("seq")
-    mine = tube_index[position]
-
-    def member(distance):
-        block = position + distance
-        return (block >= 0) & (block < count) & (tube_index[jnp.clip(block, 0, count - 1)] == mine)
-
-    flags = jnp.stack([member(distance) for distance in SLOTS])
-    blocks_open = jnp.stack([flags[1] | flags[3], True, flags[2] | flags[0]])
-    tube_bias = jnp.where(jnp.repeat(blocks_open, rows), 0.0, MASKED)
-    heads = ctrl_bias.shape[0]
-    ctrl_part = jnp.where(
-        (ctrl_owner == owner_index[position])[None, :], ctrl_bias[:, None], MASKED
-    )
-    bias = jnp.concatenate(
-        [jnp.broadcast_to(tube_bias[None, :], (heads, 3 * rows)), ctrl_part], axis=1
-    ).reshape(pairs, 2, -1)
     vmem = pl.BlockSpec(memory_space=pltpu.VMEM)
+    hbm = pl.BlockSpec(memory_space=pl.ANY)
     block = jax.ShapeDtypeStruct((rows, width), jnp.bfloat16)
     ctrl_block = jax.ShapeDtypeStruct((ctrl_rows, width), jnp.bfloat16)
     tile = (2, rows, LANES)
-    ctrl_tile = (count, 2, ctrl_rows, LANES)
+    ctrl_tile = (2, ctrl_rows, LANES)
     slots = len(SLOTS)
-    return pl.pallas_call(
+    results = pl.pallas_call(
         partial(tube_kernel, count),
         out_shape=(block, block, block, block, ctrl_block, ctrl_block),
-        in_specs=[vmem] * 7 + [pl.BlockSpec(memory_space=pltpu.SMEM)],
+        in_specs=[pl.BlockSpec(memory_space=pltpu.HBM)] * 10,
         out_specs=[vmem] * 6,
         scratch_shapes=[
+            pltpu.VMEM((rows, width), jnp.bfloat16),
+            pltpu.VMEM((rows, width), jnp.bfloat16),
             pltpu.VMEM((pairs,) + tile, jnp.bfloat16),
             pltpu.VMEM((pairs, slots) + tile, jnp.bfloat16),
-            pltpu.VMEM((pairs,) + ctrl_tile, jnp.bfloat16),
+            pltpu.VMEM((pairs, count) + ctrl_tile, jnp.bfloat16),
             pltpu.VMEM((pairs,) + tile, jnp.bfloat16),
             pltpu.VMEM((pairs, slots) + tile, jnp.bfloat16),
             pltpu.VMEM((pairs, slots) + tile, jnp.bfloat16),
-            pltpu.VMEM((pairs,) + ctrl_tile, jnp.bfloat16),
-            pltpu.VMEM((pairs,) + ctrl_tile, jnp.bfloat16),
+            pltpu.VMEM((pairs, 2, count // 2) + ctrl_tile, jnp.bfloat16),
+            pltpu.VMEM((pairs, count // 2) + ctrl_tile, jnp.bfloat16),
+            pltpu.VMEM((pairs, count // 2) + ctrl_tile, jnp.bfloat16),
+            pltpu.SMEM(ctrl_bias.shape, jnp.float32),
+            pltpu.SMEM(tube_lengths.shape, jnp.int32),
+            pltpu.SMEM(tube_owner.shape, jnp.int32),
+            pltpu.VMEM(ctrl_owner.shape, jnp.int32),
+            pltpu.SemaphoreType.DMA((pairs, 4)),
+            pltpu.SemaphoreType.DMA((6,)),
             pltpu.SemaphoreType.DMA((pairs, slots)),
             pltpu.SemaphoreType.DMA((pairs, slots)),
             pltpu.SemaphoreType.DMA((pairs, count)),
             pltpu.SemaphoreType.DMA((pairs, count)),
             pltpu.SemaphoreType.DMA((pairs, slots)),
             pltpu.SemaphoreType.DMA((pairs, slots)),
-            pltpu.SemaphoreType.DMA((pairs, count)),
-            pltpu.SemaphoreType.DMA((pairs, count)),
+            pltpu.SemaphoreType.DMA((pairs,)),
+            pltpu.SemaphoreType.DMA((pairs,)),
+            pltpu.SemaphoreType.DMA((pairs, count // 2)),
+            pltpu.SemaphoreType.DMA((pairs, count // 2)),
         ],
         compiler_params=pltpu.CompilerParams(
-            collective_id=0, has_side_effects=True, vmem_limit_bytes=48 * 1024 * 1024
+            collective_id=0, has_side_effects=True, vmem_limit_bytes=64 * 1024 * 1024 - 65536
         ),
     )(
         query_states, key_states, value_states, d_attended, ctrl_key, ctrl_value,
-        bias, flags.astype(jnp.int32),
-    )
+        ctrl_bias, tube_lengths, tube_owner, ctrl_owner,
+    )
+    return pl.pallas_call(
+        hand_over,
+        out_shape=(block, block, block, block, ctrl_block, ctrl_block),
+        in_specs=[hbm] * 6,
+        out_specs=[hbm] * 6,
+        scratch_shapes=[pltpu.SemaphoreType.DMA((6,))],
+        compiler_params=pltpu.CompilerParams(vmem_limit_bytes=64 * 1024 * 1024 - 65536),
+    )(*results)
+
+
+def hand_over(*refs):
+    sems = refs[-1]
+    copies = [
+        pltpu.make_async_copy(refs[i], refs[6 + i], sems.at[i]) for i in range(6)
+    ]
+    for copy in copies:
+        copy.start()
+    for copy in copies:
+        copy.wait()
 
 
 def fused_or_plain(*arrays):

time: 95.6 us -> 93 us (0.973); the launches traced: 94.2 us -> 92.8 us
  Pallas kernels: 74.7 us -> 92.2 us
  local copies, waits for them, and re-layouts: 10.3 us -> 0 us
  between operations: 5.93 us -> 0.64 us
  other arithmetic: 3.28 us -> 0 us
    pallas_call x0 -> x1, Pallas kernels: none -> 28 us  [fused_shards(): pl.pallas_call(hand_over, out_shape=(block, block, block, block, ctrl_blo...]
    pallas_call x1, Pallas kernels: 74.7 us -> 64.2 us  [fused_shards(): pl.pallas_call(partial(tube_kernel, count), out_shape=(block, block, bloc...]
    unnamed x18 -> x0, local copies, waits for them, and re-layouts: 8.32 us -> none
    eq x1 -> x0, other arithmetic: 1.33 us -> none  [fused_shards(): ctrl_owner == owner_index[position]]
    dynamic_slice x2 -> x0, local copies, waits for them, and re-layouts: 1.18 us -> none  [the longest x1 0.6 us: member(): tube_index[jnp.clip(block, 0, count - 1)] == mine]
where the time goes in v2:
time: 93 us; the launch traced here: 92.8 us
  Pallas kernels  92.2 us (99%)
    pallas_call x1, Pallas kernels, fused_shards(): pl.pallas_call(partial(tube_kernel, count), out_shape=(block, block, bloc...  64.2 us
    pallas_call x1, Pallas kernels, fused_shards(): pl.pallas_call(hand_over, out_shape=(block, block, block, block, ctrl_blo...  28 us

profile of v2, /device:TPU:0, one launch (start us, length us, event | category | flops | bytes accessed | tf_op | source)
XLA Modules:
  0.0 92.8 jit_solution(4068661753892048392)
XLA Ops:
  0.6 64.2 %shard_map.145 = (bf16[128,768]{1,0:T(8,128)(2,1)}, bf16[128,768]{1,0:T(8,128)(2,1)}, bf16[128,768]{1,0:T(8,128)(2,1)}, bf16[128,768]{1,0:T(8,128)(2,1)}, bf16[3...) custom-call(bf16[128,768]{1,0:T(8,128)(2,1)} %q_hbm.1, bf16[128,768]{1,0:T(8,128)(2,1)} %k_hbm.1, bf16[128,768]{1,0:T(8,128)(2,1)} %v_hbm.1, ...), custom_call_target="tpu_custom_call" | custom-call | tf_op jit(solution)/shard_map/pallas_call | solution.py:597
  64.9 28.0 %shard_map.146 = (bf16[128,768]{1,0:T(8,128)(2,1)}, bf16[128,768]{1,0:T(8,128)(2,1)}, bf16[128,768]{1,0:T(8,128)(2,1)}, bf16[128,768]{1,0:T(8,128)(2,1)}, bf16[3...) custom-call(bf16[128,768]{1,0:T(8,128)(2,1)} %get-tuple-element.12.refs_0_, bf16[128,768]{1,0:T(8,128)(2,1)} %get-tuple-element.13.refs_1_, ...), custom_call_target="tpu_custom_call" | custom-call | tf_op jit(solution)/shard_map/pallas_call | solution.py:638

commit v3 on v2

--- a/solution.py
+++ b/solution.py
@@ -640,19 +640,26 @@
         out_shape=(block, block, block, block, ctrl_block, ctrl_block),
         in_specs=[hbm] * 6,
         out_specs=[hbm] * 6,
-        scratch_shapes=[pltpu.SemaphoreType.DMA((6,))],
+        scratch_shapes=[pltpu.VMEM(result.shape, result.dtype) for result in results]
+        + [pltpu.SemaphoreType.DMA((6,)), pltpu.SemaphoreType.DMA((6,))],
         compiler_params=pltpu.CompilerParams(vmem_limit_bytes=64 * 1024 * 1024 - 65536),
     )(*results)
 
 
 def hand_over(*refs):
-    sems = refs[-1]
-    copies = [
-        pltpu.make_async_copy(refs[i], refs[6 + i], sems.at[i]) for i in range(6)
+    loaded, load_sems, store_sems = refs[12:18], refs[18], refs[19]
+    copies_in = [
+        pltpu.make_async_copy(refs[i], loaded[i], load_sems.at[i]) for i in range(6)
     ]
-    for copy in copies:
+    copies_out = [
+        pltpu.make_async_copy(loaded[i], refs[6 + i], store_sems.at[i]) for i in range(6)
+    ]
+    for copy in copies_in:
         copy.start()
-    for copy in copies:
+    for copy_in, copy_out in zip(copies_in, copies_out):
+        copy_in.wait()
+        copy_out.start()
+    for copy in copies_out:
         copy.wait()
 
 

time: 93 us -> 67.1 us (0.72)
  Pallas kernels: 92.2 us -> 66.3 us
    pallas_call x1, Pallas kernels: 28 us -> 2.02 us  [fused_shards(): pl.pallas_call(hand_over, out_shape=(block, block, block, block, ctrl_blo...]
where the time goes in v3:
time: 67.1 us; the launch traced here: 66.9 us
  Pallas kernels  66.3 us (99%)
    pallas_call x1, Pallas kernels, fused_shards(): pl.pallas_call(partial(tube_kernel, count), out_shape=(block, block, bloc...  64.2 us
    pallas_call x1, Pallas kernels, fused_shards(): pl.pallas_call(hand_over, out_shape=(block, block, block, block, ctrl_blo...  2.02 us

profile of v3, /device:TPU:0, one launch (start us, length us, event | category | flops | bytes accessed | tf_op | source)
XLA Modules:
  0.0 66.9 jit_solution(9822799039107577550)
XLA Ops:
  0.6 64.2 %shard_map.145 = (bf16[128,768]{1,0:T(8,128)(2,1)}, bf16[128,768]{1,0:T(8,128)(2,1)}, bf16[128,768]{1,0:T(8,128)(2,1)}, bf16[128,768]{1,0:T(8,128)(2,1)}, bf16[3...) custom-call(bf16[128,768]{1,0:T(8,128)(2,1)} %q_hbm.1, bf16[128,768]{1,0:T(8,128)(2,1)} %k_hbm.1, bf16[128,768]{1,0:T(8,128)(2,1)} %v_hbm.1, ...), custom_call_target="tpu_custom_call" | custom-call | tf_op jit(solution)/shard_map/pallas_call | solution.py:597
  64.9 2.0 %shard_map.146 = (bf16[128,768]{1,0:T(8,128)(2,1)}, bf16[128,768]{1,0:T(8,128)(2,1)}, bf16[128,768]{1,0:T(8,128)(2,1)}, bf16[128,768]{1,0:T(8,128)(2,1)}, bf16[3...) custom-call(bf16[128,768]{1,0:T(8,128)(2,1)} %get-tuple-element.12.refs_0_, bf16[128,768]{1,0:T(8,128)(2,1)} %get-tuple-element.13.refs_1_, ...), custom_call_target="tpu_custom_call" | custom-call | tf_op jit(solution)/shard_map/pallas_call | solution.py:638

commit v4 on v3

--- a/solution.py
+++ b/solution.py
@@ -275,14 +275,16 @@
     count, q_hbm, k_hbm, v_hbm, g_hbm, ck_hbm, cv_hbm,
     bias_hbm, length_hbm, owner_hbm, tag_hbm,
     att_ref, dq_ref, dk_ref, dv_ref, dck_ref, dcv_ref,
-    q_ref, g_ref, own, window, ctrl, own_grad, grad_out, grad_in, ctrl_out, ctrl_mid, ctrl_in,
+    q_ref, g_ref, own, window, ctrl, own_grad, grad_out, grad_mid, grad_in, ctrl_out, ctrl_mid, ctrl_in,
     bias_ref, length_ref, owner_ref, tag_ref, load_sem, query_sem,
     kv_send, kv_recv, ctrl_send, ctrl_recv, grad_send, grad_recv,
-    mid_send, mid_recv, sum_send, sum_recv,
+    mid_send, mid_recv, sum_send, sum_recv, part_send, part_recv,
 ):
     me = lax.axis_index("seq")
     column = lax.rem(me, 2)
-    peer = me + 1 - 2 * column
+    side = 1 - 2 * column
+    peer = me + side
+    near, across, far, back = 2 - column, 1 + column, 3 - 3 * column, 3 * column
     level = me // 2
     levels = count // 2
     rows = q_ref.shape[0]
@@ -296,18 +298,51 @@
     def columns(pair):
         return pl.ds(pl.multiple_of(pair * LANES, LANES), LANES)
 
-    def kv_copy(pair, slot):
+    def kv_copy(pair, slot, distance):
         return pltpu.make_async_remote_copy(
             own.at[pair], window.at[pair, slot], kv_send.at[pair, slot], kv_recv.at[pair, slot],
-            device_id={"seq": me - SLOTS[slot]}, device_id_type=MESH,
-        )
-
-    def grad_copy(pair, slot):
+            device_id={"seq": me - distance}, device_id_type=MESH,
+        )
+
+    def kv_arrival(pair, slot):
+        return kv_copy(pair, slot, -side)
+
+    def kv_onward(pair, by_peer):
+        source, target = (far, near) if by_peer else (near, across)
+        return pltpu.make_async_remote_copy(
+            window.at[pair, source], window.at[pair, target],
+            kv_send.at[pair, near], kv_recv.at[pair, target],
+            device_id={"seq": peer if by_peer else me + 2 * side}, device_id_type=MESH,
+        )
+
+    def grad_copy(pair, slot, distance):
         return pltpu.make_async_remote_copy(
             grad_out.at[pair, slot], grad_in.at[pair, slot],
             grad_send.at[pair, slot], grad_recv.at[pair, slot],
-            device_id={"seq": me + SLOTS[slot]}, device_id_type=MESH,
-        )
+            device_id={"seq": me + distance}, device_id_type=MESH,
+        )
+
+    def grad_arrival(pair, slot):
+        return grad_copy(pair, slot, side)
+
+    def part_copy(pair, by_peer):
+        return pltpu.make_async_remote_copy(
+            grad_out.at[pair, across], grad_mid.at[pair], part_send.at[pair], part_recv.at[pair],
+            device_id={"seq": peer if by_peer else me - 2 * side}, device_id_type=MESH,
+        )
+
+    has_far, has_back = inside(me + 2 * side), inside(me - 2 * side)
+
+    def by_parity(pair, act):
+        even = lax.rem(pair, 2) == 0
+
+        @pl.when(even)
+        def _():
+            act(True)
+
+        @pl.when(jnp.logical_not(even))
+        def _():
+            act(False)
 
     def mate(step):
         return lax.rem(me + 2 * step, count)
@@ -399,7 +434,7 @@
         def _():
             window[:, slot] = jnp.zeros((pairs,) + window.shape[2:], window.dtype)
 
-        @pl.when(jnp.logical_not(inside(me - distance)))
+        @pl.when(jnp.logical_not(inside(me - distance)) | (near == slot))
         def _():
             grad_in[:, slot] = jnp.zeros((pairs,) + grad_in.shape[2:], grad_in.dtype)
 
@@ -413,12 +448,18 @@
     def send(pair, _):
         for copy in loads(pair):
             copy.wait()
+        kv_copy(pair, across, -side).start()
+
+        @pl.when(has_far)
+        def _():
+            kv_copy(pair, back, -2 * side).start()
+
+        @pl.when(has_back)
+        def _():
+            kv_copy(pair, far, 2 * side).start()
+
         for step in range(levels):
             ctrl_copy(pair, step).start()
-        for slot, distance in enumerate(SLOTS):
-            @pl.when(inside(me - distance))
-            def _():
-                kv_copy(pair, slot).start()
         return 0
 
     lax.fori_loop(0, pairs, send, 0)
@@ -454,6 +495,18 @@
         for step in range(1, levels):
             ctrl_arrival(pair, step).wait_recv()
             ctrl_onward(pair, step).start()
+
+        def act(by_peer):
+            if not by_peer:
+                kv_arrival(pair, near).wait_recv()
+
+            @pl.when(has_far)
+            def _():
+                if by_peer:
+                    kv_arrival(pair, far).wait_recv()
+                kv_onward(pair, by_peer).start()
+
+        by_parity(pair, act)
 
     def column_sums(pair):
         mid_copy(pair).wait()
@@ -463,6 +516,25 @@
         for step in range(1, levels):
             sum_copy(pair, step).start()
 
+        def act(by_peer):
+            slot = far if by_peer else near
+
+            @pl.when(has_far)
+            def _():
+                part_copy(pair, True).wait_recv()
+                grad_out[pair, slot] = (
+                    grad_out[pair, slot].astype(jnp.float32) + grad_mid[pair].astype(jnp.float32)
+                ).astype(jnp.bfloat16)
+
+            if by_peer:
+                @pl.when(has_far)
+                def _():
+                    grad_copy(pair, far, 2 * side).start()
+            else:
+                grad_copy(pair, near, side).start()
+
+        by_parity(pair, act)
+
     def work(pair, _):
         @pl.when(pair + AHEAD < pairs)
         def _():
@@ -471,10 +543,20 @@
         ctrl_arrival(pair, 0).wait_recv()
         for step in range(1, levels):
             ctrl_onward_arrival(pair, step).wait_recv()
-        for slot, distance in enumerate(SLOTS):
-            @pl.when(inside(me + distance))
-            def _():
-                kv_copy(pair, slot).wait_recv()
+        def await_rest(by_peer):
+            if by_peer:
+                kv_arrival(pair, near).wait_recv()
+            else:
+                @pl.when(has_far)
+                def _():
+                    kv_arrival(pair, far).wait_recv()
+
+        by_parity(pair, await_rest)
+
+        @pl.when(has_back)
+        def _():
+            kv_arrival(pair, back).wait_recv()
+            kv_arrival(pair, across).wait_recv()
 
         def gathered(kind):
             first = jnp.where(
@@ -523,10 +605,21 @@
                     shared[device * ctrl_rows : (device + 1) * ctrl_rows]
                 )
         mid_copy(pair).start()
-        for slot, distance in enumerate(SLOTS):
-            @pl.when(inside(me + distance))
+
+        def hand_on(by_peer):
+            @pl.when(has_back)
             def _():
-                grad_copy(pair, slot).start()
+                part_copy(pair, by_peer).start()
+                grad_copy(pair, back, -2 * side).start()
+
+            if by_peer:
+                grad_copy(pair, near, side).start()
+            else:
+                @pl.when(has_far)
+                def _():
+                    grad_copy(pair, far, 2 * side).start()
+
+        by_parity(pair, hand_on)
 
         @pl.when(pair > 0)
         def _():
@@ -543,10 +636,16 @@
         ctrl_in[pair, level] = ctrl_out[pair, column, level]
         for step in range(1, levels):
             sum_arrival(pair, step).wait_recv()
-        for slot, distance in enumerate(SLOTS):
-            @pl.when(inside(me - distance))
-            def _():
-                grad_copy(pair, slot).wait_recv()
+        grad_arrival(pair, across).wait_recv()
+
+        @pl.when(has_back)
+        def _():
+            grad_arrival(pair, far).wait_recv()
+
+        @pl.when(has_far)
+        def _():
+            grad_arrival(pair, back).wait_recv()
+
         for kind, (key_ref, ctrl_ref) in enumerate(((dk_ref, dck_ref), (dv_ref, dcv_ref))):
             total = own_grad[pair, kind].astype(jnp.float32)
             for slot in range(len(SLOTS)):
@@ -566,14 +665,21 @@
         for step in range(1, levels):
             ctrl_onward(pair, step).wait_send()
             sum_copy(pair, step).wait_send()
-        for slot, distance in enumerate(SLOTS):
-            @pl.when(inside(me - distance))
-            def _():
-                kv_copy(pair, slot).wait_send()
-
-            @pl.when(inside(me + distance))
-            def _():
-                grad_copy(pair, slot).wait_send()
+        kv_copy(pair, across, -side).wait_send()
+        grad_copy(pair, near, side).wait_send()
+
+        @pl.when(has_far)
+        def _():
+            kv_copy(pair, back, -2 * side).wait_send()
+            kv_onward(pair, True).wait_send()
+            grad_copy(pair, far, 2 * side).wait_send()
+
+        @pl.when(has_back)
+        def _():
+            kv_copy(pair, far, 2 * side).wait_send()
+            part_copy(pair, True).wait_send()
+            grad_copy(pair, back, -2 * side).wait_send()
+
         return 0
 
     lax.fori_loop(0, pairs, drain, 0)
@@ -607,6 +713,7 @@
             pltpu.VMEM((pairs, count) + ctrl_tile, jnp.bfloat16),
             pltpu.VMEM((pairs,) + tile, jnp.bfloat16),
             pltpu.VMEM((pairs, slots) + tile, jnp.bfloat16),
+            pltpu.VMEM((pairs,) + tile, jnp.bfloat16),
             pltpu.VMEM((pairs, slots) + tile, jnp.bfloat16),
             pltpu.VMEM((pairs, 2, count // 2) + ctrl_tile, jnp.bfloat16),
             pltpu.VMEM((pairs, count // 2) + ctrl_tile, jnp.bfloat16),
@@ -627,6 +734,8 @@
             pltpu.SemaphoreType.DMA((pairs,)),
             pltpu.SemaphoreType.DMA((pairs, count // 2)),
             pltpu.SemaphoreType.DMA((pairs, count // 2)),
+            pltpu.SemaphoreType.DMA((pairs,)),
+            pltpu.SemaphoreType.DMA((pairs,)),
         ],
         compiler_params=pltpu.CompilerParams(
             collective_id=0, has_side_effects=True, vmem_limit_bytes=64 * 1024 * 1024 - 65536

time: 67.1 us -> 57.3 us (0.85)
  Pallas kernels: 66.3 us -> 56.5 us
    pallas_call x1, Pallas kernels: 64.2 us -> 54.5 us  [fused_shards(): pl.pallas_call(partial(tube_kernel, count), out_shape=(block, block, bloc...]
where the time goes in v4:
time: 57.3 us; the launch traced here: 57.2 us
  Pallas kernels  56.5 us (99%)
  between operations  0.64 us (1%)
    pallas_call x1, Pallas kernels, fused_shards(): pl.pallas_call(partial(tube_kernel, count), out_shape=(block, block, bloc...  54.5 us
    pallas_call x1, Pallas kernels, fused_shards(): pl.pallas_call(hand_over, out_shape=(block, block, block, block, ctrl_blo...  2.02 us

profile of v4, /device:TPU:0, one launch (start us, length us, event | category | flops | bytes accessed | tf_op | source)
XLA Modules:
  0.0 57.2 jit_solution(3321951403409684231)
XLA Ops:
  0.6 54.5 %shard_map.145 = (bf16[128,768]{1,0:T(8,128)(2,1)}, bf16[128,768]{1,0:T(8,128)(2,1)}, bf16[128,768]{1,0:T(8,128)(2,1)}, bf16[128,768]{1,0:T(8,128)(2,1)}, bf16[3...) custom-call(bf16[128,768]{1,0:T(8,128)(2,1)} %q_hbm.1, bf16[128,768]{1,0:T(8,128)(2,1)} %k_hbm.1, bf16[128,768]{1,0:T(8,128)(2,1)} %v_hbm.1, ...), custom_call_target="tpu_custom_call" | custom-call | tf_op jit(solution)/shard_map/pallas_call | solution.py:703
  55.1 2.0 %shard_map.146 = (bf16[128,768]{1,0:T(8,128)(2,1)}, bf16[128,768]{1,0:T(8,128)(2,1)}, bf16[128,768]{1,0:T(8,128)(2,1)}, bf16[128,768]{1,0:T(8,128)(2,1)}, bf16[3...) custom-call(bf16[128,768]{1,0:T(8,128)(2,1)} %get-tuple-element.12.refs_0_, bf16[128,768]{1,0:T(8,128)(2,1)} %get-tuple-element.13.refs_1_, ...), custom_call_target="tpu_custom_call" | custom-call | tf_op jit(solution)/shard_map/pallas_call | solution.py:747

commit v5 on v4

--- a/solution.py
+++ b/solution.py
@@ -334,7 +334,7 @@
     has_far, has_back = inside(me + 2 * side), inside(me - 2 * side)
 
     def by_parity(pair, act):
-        even = lax.rem(pair, 2) == 0
+        even = lax.rem(pair, 3) == 0
 
         @pl.when(even)
         def _():
@@ -439,11 +439,9 @@
             grad_in[:, slot] = jnp.zeros((pairs,) + grad_in.shape[2:], grad_in.dtype)
 
     barrier = pltpu.get_barrier_semaphore()
-    for step in range(1, count):
-        pl.semaphore_signal(
-            barrier, inc=1, device_id={"seq": lax.rem(me + step, count)}, device_id_type=MESH
-        )
-    pl.semaphore_wait(barrier, count - 1)
+    for partner in [peer] + [mate(step) for step in range(1, levels)]:
+        pl.semaphore_signal(barrier, inc=1, device_id={"seq": partner}, device_id_type=MESH)
+    pl.semaphore_wait(barrier, levels)
 
     def send(pair, _):
         for copy in loads(pair):

time: 57.3 us -> 54.5 us (0.951)
  Pallas kernels: 56.5 us -> 53.7 us
    pallas_call x1, Pallas kernels: 54.5 us -> 51.7 us  [fused_shards(): pl.pallas_call(partial(tube_kernel, count), out_shape=(block, block, bloc...]
where the time goes in v5:
time: 54.5 us; the launch traced here: 54.3 us
  Pallas kernels  53.7 us (99%)
  between operations  0.64 us (1%)
    pallas_call x1, Pallas kernels, fused_shards(): pl.pallas_call(partial(tube_kernel, count), out_shape=(block, block, bloc...  51.7 us
    pallas_call x1, Pallas kernels, fused_shards(): pl.pallas_call(hand_over, out_shape=(block, block, block, block, ctrl_blo...  2.02 us

profile of v5, /device:TPU:0, one launch (start us, length us, event | category | flops | bytes accessed | tf_op | source)
XLA Modules:
  0.0 54.3 jit_solution(2905507113120965753)
XLA Ops:
  0.6 51.7 %shard_map.145 = (bf16[128,768]{1,0:T(8,128)(2,1)}, bf16[128,768]{1,0:T(8,128)(2,1)}, bf16[128,768]{1,0:T(8,128)(2,1)}, bf16[128,768]{1,0:T(8,128)(2,1)}, bf16[3...) custom-call(bf16[128,768]{1,0:T(8,128)(2,1)} %q_hbm.1, bf16[128,768]{1,0:T(8,128)(2,1)} %k_hbm.1, bf16[128,768]{1,0:T(8,128)(2,1)} %v_hbm.1, ...), custom_call_target="tpu_custom_call" | custom-call | tf_op jit(solution)/shard_map/pallas_call | solution.py:701
  52.3 2.0 %shard_map.146 = (bf16[128,768]{1,0:T(8,128)(2,1)}, bf16[128,768]{1,0:T(8,128)(2,1)}, bf16[128,768]{1,0:T(8,128)(2,1)}, bf16[128,768]{1,0:T(8,128)(2,1)}, bf16[3...) custom-call(bf16[128,768]{1,0:T(8,128)(2,1)} %get-tuple-element.12.refs_0_, bf16[128,768]{1,0:T(8,128)(2,1)} %get-tuple-element.13.refs_1_, ...), custom_call_target="tpu_custom_call" | custom-call | tf_op jit(solution)/shard_map/pallas_call | solution.py:745
